TPU v7x, 32 devices: a whole 2x2x4 slice. The times are simulated.
32 devices in a mesh: dom: 8 (over z, x), ref: 4 (over y, core).
Axes of the slice: x: 2, y: 2, z: 4, core: 2. Of those that a mesh axis runs over, the one named last changes fastest.
Arguments:
- particles: float32 [1024, 128], P('dom'), may hold values from -1.2 to 1.2
- references: float32 [4096, 128], P('ref'), may hold values from -1 to 1.2
Outputs:
- moved: float32 [1024, 128], P(('dom', 'ref'))
- drift: float32 [1024, 128], P(('dom', 'ref'))
All inputs are finite; a program needn't handle non-finite values.
Results may differ from a plain program's by a relative error of at most 0.00035.
Values sent between devices are 32-bit elements; how exact they have to be, the bound alone decides.
No kernel may reach another device: no remote copies, remote signals or barrier semaphores. Data moves between devices by JAX's collectives and lax.ppermute only.
A program may use at most 64 MiB of HBM per device.

v0:
```python
import jax
import jax.numpy as jnp
from jax import lax
from jax.sharding import PartitionSpec as P

STEPS = 2


step_size = 0.5


def kernel_terms(block, others):
    inner = jnp.dot(
        block, others.T, precision=lax.Precision.HIGHEST, preferred_element_type=jnp.float32
    )
    squared = (
        jnp.sum(block * block, axis=1)[:, None]
        + jnp.sum(others * others, axis=1)[None, :]
        - 2.0 * inner
    )
    weights = jnp.exp(-0.5 * squared)
    pulled = jnp.dot(
        weights, others, precision=lax.Precision.HIGHEST, preferred_element_type=jnp.float32
    )
    return (pulled, jnp.sum(weights, axis=1))


def partial_gradient(block, own_rows, references, count_p, count_r):
    pulled, summed = kernel_terms(block, lax.all_gather(own_rows, "dom", axis=0, tiled=True))
    pull_r, sum_r = kernel_terms(block, references)
    return (pulled - summed[:, None] * block) / count_p - (
        pull_r - sum_r[:, None] * block
    ) / count_r


def on_device(particles, references):
    n_ref = lax.axis_size("ref")
    n_dom = lax.axis_size("dom")
    rows = particles.shape[0] // n_ref
    count_p = particles.shape[0] * n_dom
    count_r = references.shape[0] * n_ref
    offset = lax.axis_index("ref") * rows
    start_rows = lax.dynamic_slice_in_dim(particles, offset, rows, 0)
    block = particles
    own_rows = start_rows
    for step in range(STEPS):
        partial_value = partial_gradient(block, own_rows, references, count_p, count_r)
        share = lax.psum_scatter(partial_value, "ref", scatter_dimension=0, tiled=True)
        own_rows = own_rows - step_size * share
        if step + 1 < STEPS:
            block = lax.all_gather(own_rows, "ref", axis=0, tiled=True)
    return (own_rows, (own_rows - start_rows) / step_size)


def solution(mesh):
    placed = (P("dom", None), P("ref", None))
    return jax.shard_map(
        on_device,
        mesh=mesh,
        in_specs=placed,
        out_specs=(P(("dom", "ref"), None), P(("dom", "ref"), None)),
        check_vma=False,
    )
```

profile of v0, /device:TPU:0, one launch (start us, length us, event | category | flops | bytes accessed | tf_op | source)
XLA Modules:
  0.0 132.5 jit_solution(5655640361092528727)
XLA Ops:
  7.2 0.0 reduce-scatter.3.cloned.1.call-start
  7.2 0.0 copy-start.1
  7.2 1.0 multiply_reduce_fusion.4
  8.2 0.0 copy-start
  8.2 1.3 multiply_reduce_fusion
  9.6 0.0 copy-done.1
  9.6 32.3 %all_gather.9 = f32[256,128]{1,0:T(8,128)S(1)} all-gather(f32[32,128]{1,0:T(8,128)S(1)} %constant_dynamic-slice_fusion), channel_id=1, replica_groups=mesh['dom'=8,'ref'=4] {'dom'}, dimensions={0}, use_global_device_ids=true | all-gather | bytes 147456 | tf_op jit(solution)/shard_map/all_gather | solution.py:29
  41.9 0.1 multiply_reduce_fusion.2
  42.0 0.3 fusion.19
  42.3 0.0 copy-done
  42.3 0.8 fusion.20
  43.1 0.4 fusion.17
  43.5 1.3 fusion.16
  44.8 0.0 reduce-scatter.3.cloned.1.call-update
  44.8 0.0 reduce-scatter.5.cloned.1.call-start
  44.9 20.5 %reduce-scatter.3.cloned.1.call-done = f32[32,128]{1,0:T(8,128)} async-done(((f32[128,128]{1,0:T(8,128)}), f32[32,128]{1,0:T(8,128)}) %reduce-scatter.3.cloned.1.call-update) | async-done | bytes 16400 | tf_op jit(solution)/shard_map/reduce_scatter | solution.py:48
  65.3 0.7 multiply_subtract_fusion.1
  66.0 5.2 %all_gather.10 = f32[128,128]{1,0:T(8,128)S(1)} all-gather(f32[32,128]{1,0:T(8,128)S(1)} %multiply_subtract_fusion.1), channel_id=1, replica_groups=mesh['dom'=8,'ref'=4] {'ref'}, dimensions={0}, use_global_device_ids=true | all-gather | bytes 81920 | tf_op jit(solution)/shard_map/all_gather | solution.py:51
  71.3 30.6 %all_gather.11 = f32[256,128]{1,0:T(8,128)S(1)} all-gather(f32[32,128]{1,0:T(8,128)S(1)} %multiply_subtract_fusion.1), channel_id=1, replica_groups=mesh['dom'=8,'ref'=4] {'dom'}, dimensions={0}, use_global_device_ids=true | all-gather | bytes 147456 | tf_op jit(solution)/shard_map/all_gather | solution.py:29
  101.8 0.1 multiply_reduce_fusion.3
  102.0 0.1 multiply_reduce_fusion.1
  102.1 0.8 fusion.22
  102.8 0.3 fusion.21
  103.2 0.4 fusion.18
  103.6 1.3 fusion.14
  104.8 0.0 reduce-scatter.5.cloned.1.call-update
  104.9 19.5 %reduce-scatter.5.cloned.1.call-done = f32[32,128]{1,0:T(8,128)} async-done(((f32[128,128]{1,0:T(8,128)}), f32[32,128]{1,0:T(8,128)}) %reduce-scatter.5.cloned.1.call-update) | async-done | bytes 16400 | tf_op jit(solution)/shard_map/reduce_scatter | solution.py:48
  124.4 1.3 %subtract_multiply_fusion = (f32[32,128]{1,0:T(8,128)}, f32[32,128]{1,0:T(8,128)}) fusion(f32[32,128]{1,0:T(8,128)S(1)} %multiply_subtract_fusion.1, f32[32,128]{1,0:T(8,128)} %reduce-scatter.5.cloned.1.call-done, f32[128,128]{1,0:T(8,128)S(1)} %copy-done.1, s32[]{:T(128)S(6)} %select_n.3), kind=kLoop, calls=%fused_computation.32 | loop fusion | flops 16384 | bytes 81924 | tf_op jit(solution)/shard_map/div | solution.py:52
  (1 shorter events, 0.0 us)
Async XLA Ops:
  7.2 58.2 %reduce-scatter.3.cloned.1.call-start = ((), (), s32[]{:S(2)}) async-start(), calls=%async_computation.2 | async-start | bytes 81920 | tf_op jit(solution)/shard_map/reduce_scatter | solution.py:48
  7.2 2.4 %copy-start.1 = (f32[128,128]{1,0:T(8,128)S(1)}, f32[128,128]{1,0:T(8,128)}, u32[]{:S(2)}) copy-start(f32[128,128]{1,0:T(8,128)} %param.2) | copy-start | bytes 196612
  8.2 34.1 %copy-start = (f32[1024,128]{1,0:T(8,128)S(1)}, f32[1024,128]{1,0:T(8,128)}, u32[]{:S(2)}) copy-start(f32[1024,128]{1,0:T(8,128)} %param.3) | copy-start | bytes 1572868
  44.8 79.6 %reduce-scatter.5.cloned.1.call-start = ((), (), s32[]{:S(2)}) async-start(), calls=%async_computation.3 | async-start | bytes 81920 | tf_op jit(solution)/shard_map/reduce_scatter | solution.py:48
Sparse Core Ops, SparseCore 0:
  44.9 20.3 reduce-scatter.2
  105.0 19.3 reduce-scatter.4
where the time goes:
time: 133 us
  blocking collectives  68.1 us (51%)
  waiting for transfers between devices  40 us (30%)
  between operations  14.1 us (11%)
  matrix products  5.5 us (4%)
  other arithmetic  4.71 us (4%)
    all_gather x2, blocking collectives, partial_gradient(): lax.all_gather(own_rows, 'dom', axis=0, tiled=True)  62.9 us
    reduce_scatter x2, waiting for transfers between devices, on_device(): lax.psum_scatter(partial_value, 'ref', scatter_dimension=0, tiled=True)  40 us
    all_gather x1, blocking collectives, on_device(): block = lax.all_gather(own_rows, 'ref', axis=0, tiled=True)  5.23 us
    dot_general x4, matrix products, kernel_terms(): jnp.dot(weights, others, precision=lax.Precision.HIGHEST, preferred_eleme...  3.34 us
  transfers between devices with their start and end apart: 2, of which 2 were waited for; matrix products, arithmetic and copies ran while one was open for 0% of the time, Pallas kernels for 0%

commit v1 on v0

v1 whole, which is shorter than its diff:
```python
import functools

import jax
import jax.numpy as jnp
from jax import lax
from jax.experimental import pallas as pl
from jax.experimental.pallas import tpu as pltpu
from jax.sharding import PartitionSpec as P

STEPS = 2


step_size = 0.5
LOG2E = 1.4426950408889634
TILE = 1024
OVER_WIDTH = (((1,), (1,)), ((), ()))


def split(values):
    high = values.astype(jnp.bfloat16)
    return high, (values - high.astype(jnp.float32)).astype(jnp.bfloat16)


def left_operand(block):
    high, low = split(block * LOG2E)
    return jnp.concatenate(
        [jnp.concatenate([high, high], axis=1), jnp.concatenate([low, low], axis=1)], axis=0
    )


def kernel_terms(left, left_square, others):
    rows = left.shape[0] // 2
    width = others.shape[1]
    high, low = split(others)
    right = jnp.concatenate([high, low], axis=1)
    square = jnp.transpose(jnp.sum(others * others, axis=1, keepdims=True)) * (-0.5 * LOG2E)
    both = lax.dot_general(left, right, OVER_WIDTH, preferred_element_type=jnp.float32)
    weights = jnp.exp2(both[:rows] + both[rows:] + (left_square + square))
    weights_high, weights_low = split(weights)
    pulled = jnp.dot(
        jnp.concatenate([weights_high, weights_low], axis=0), right, preferred_element_type=jnp.float32
    )
    pulled = pulled[:rows] + pulled[rows:]
    return pulled[:, :width] + pulled[:, width:], jnp.sum(weights, axis=1, keepdims=True)


def all_terms(block, others_ref):
    left = left_operand(block)
    left_square = jnp.sum(block * block, axis=1, keepdims=True) * (-0.5 * LOG2E)
    count = others_ref.shape[0]
    tile = min(TILE, count)
    pulled = jnp.zeros(block.shape, jnp.float32)
    summed = jnp.zeros((block.shape[0], 1), jnp.float32)
    for start in range(0, count, tile):
        more = kernel_terms(left, left_square, others_ref[pl.ds(start, tile), :])
        pulled, summed = pulled + more[0], summed + more[1]
    return pulled - summed * block


def references_kernel(count_r, block_ref, others_ref, out_ref):
    out_ref[...] = all_terms(block_ref[...], others_ref) * (-1.0 / count_r)


def partners_kernel(count_p, block_ref, first_ref, *refs):
    other_refs, out_ref = refs[:-1], refs[-1]
    total = first_ref[...]
    for other in other_refs:
        total += all_terms(block_ref[...], other) * (1.0 / count_p)
    out_ref[...] = total


def on_vmem(body, rows, *args):
    return pl.pallas_call(
        body,
        out_shape=jax.ShapeDtypeStruct((rows, args[0].shape[1]), jnp.float32),
        in_specs=[pl.BlockSpec(memory_space=pltpu.VMEM)] * len(args),
        out_specs=pl.BlockSpec(memory_space=pltpu.VMEM),
        compiler_params=pltpu.CompilerParams(vmem_limit_bytes=40 << 20),
        cost_estimate=pl.CostEstimate(
            flops=8 * rows * args[1].shape[0] * args[0].shape[1],
            bytes_accessed=4 * sum(a.size for a in args),
            transcendentals=rows * args[1].shape[0],
        ),
    )(*args)


def exchange(values, axis, offset):
    size = lax.axis_size(axis)
    return lax.ppermute(values, axis, [(i, i ^ offset) for i in range(size)])


def offsets_of(n_dom, n_ref):
    share = n_dom // n_ref
    order = [0, 2, 1, 3] if n_ref == 4 else list(range(n_ref))
    return [[order[r] * share + i for i in range(share)] for r in range(n_ref)]


def partner_blocks(block, n_dom, n_ref):
    offsets = offsets_of(n_dom, n_ref)
    blocks = []
    for i in range(n_dom // n_ref):
        pairs = [
            (d * n_ref + r, (d ^ offsets[r][i]) * n_ref + r)
            for d in range(n_dom)
            for r in range(n_ref)
            if offsets[r][i]
        ]
        came = lax.ppermute(block, ("dom", "ref"), pairs)
        own = [r for r in range(n_ref) if not offsets[r][i]]
        if own:
            came = jnp.where(lax.axis_index("ref") == own[0], block, came)
        blocks.append(came)
    return blocks


def on_device(particles, references):
    n_ref = lax.axis_size("ref")
    n_dom = lax.axis_size("dom")
    block_rows = particles.shape[0]
    rows = block_rows // n_ref
    count_p = block_rows * n_dom
    count_r = references.shape[0] * n_ref
    place = lax.axis_index("ref")
    start_rows = lax.dynamic_slice_in_dim(particles, place * rows, rows, 0)
    block = particles
    for step in range(STEPS):
        partners = partner_blocks(block, n_dom, n_ref)
        partial_value = on_vmem(
            functools.partial(references_kernel, count_r), block_rows, block, references
        )
        partial_value = on_vmem(
            functools.partial(partners_kernel, count_p), block_rows, block, partial_value, *partners
        )
        if step + 1 < STEPS:
            offset = 1
            while offset < n_ref:
                partial_value = partial_value + exchange(partial_value, "ref", offset)
                offset *= 2
            block = block - step_size * partial_value
        else:
            total = lax.dynamic_slice_in_dim(partial_value, place * rows, rows, 0)
            for offset in range(1, n_ref):
                chunk = lax.dynamic_slice_in_dim(partial_value, (place ^ offset) * rows, rows, 0)
                total = total + exchange(chunk, "ref", offset)
            own_rows = lax.dynamic_slice_in_dim(block, place * rows, rows, 0)
            own_rows = own_rows - step_size * total
    return (own_rows, (own_rows - start_rows) / step_size)


def solution(mesh):
    placed = (P("dom", None), P("ref", None))
    return jax.shard_map(
        on_device,
        mesh=mesh,
        in_specs=placed,
        out_specs=(P(("dom", "ref"), None), P(("dom", "ref"), None)),
        check_vma=False,
    )
```

time: 133 us -> 35.8 us (0.27)
  blocking collectives: 68.1 us -> 0 us
  waiting for transfers between devices: 40 us -> 8.68 us
  starting transfers between devices: 0.08 us -> 20.3 us
  between operations: 14.1 us -> 0.76 us
  matrix products: 5.5 us -> 0 us
  other arithmetic: 4.71 us -> 1.38 us
  Pallas kernels: 0 us -> 2.55 us
  local copies, waits for them, and re-layouts: 0.02 us -> 1.9 us
    all_gather x3 -> x0, blocking collectives: 68.1 us -> none  [the longest x2 62.9 us: partial_gradient(): lax.all_gather(own_rows, 'dom', axis=0, tiled=True)]
    reduce_scatter x2 -> x0, waiting for transfers between devices: 40 us -> none  [on_device(): lax.psum_scatter(partial_value, 'ref', scatter_dimension=0, tiled=True)]
    ppermute x0 -> x9, starting transfers between devices: none -> 20.3 us  [the longest x5 14.4 us: exchange(): return lax.ppermute(values, axis, [(i, i ^ offset) for i in range(size)])]
    ppermute x0 -> x9, waiting for transfers between devices: none -> 8.68 us  [the longest x5 6.61 us: exchange(): return lax.ppermute(values, axis, [(i, i ^ offset) for i in range(size)])]
    dot_general x8 -> x0, matrix products: 5.5 us -> none  [the longest x4 3.34 us: kernel_terms(): jnp.dot(weights, others, precision=lax.Precision.HIGHEST, preferred_eleme...]
    reduce_sum x5 -> x0, other arithmetic: 2.66 us -> none  [the longest x3 1.55 us: kernel_terms(): jnp.sum(others * others, axis=1)[None, :]]
    pallas_call x0 -> x4, Pallas kernels: none -> 2.55 us  [on_vmem(): pl.pallas_call(body, out_shape=jax.ShapeDtypeStruct((rows, args[0].shape[...]
    unnamed x4 -> x6, local copies, waits for them, and re-layouts: 0.01 us -> 1.89 us
  transfers between devices with their start and end apart: 2 -> 9, of which waited for: 2 -> 5; matrix products, arithmetic and copies ran while one was open for 0% -> 0% of each run, Pallas kernels for 0% -> 4%
where the time goes in v1:
time: 35.8 us; the launch traced here: 35.6 us
  starting transfers between devices  20.3 us (57%)
  waiting for transfers between devices  8.68 us (24%)
  Pallas kernels  2.55 us (7%)
  local copies, waits for them, and re-layouts  1.9 us (5%)
  other arithmetic  1.38 us (4%)
  between operations  0.76 us (2%)
    ppermute x5, starting transfers between devices, exchange(): return lax.ppermute(values, axis, [(i, i ^ offset) for i in range(size)])  14.4 us
    ppermute x5, waiting for transfers between devices, exchange(): return lax.ppermute(values, axis, [(i, i ^ offset) for i in range(size)])  6.61 us
    ppermute x4, starting transfers between devices, partner_blocks(): came = lax.ppermute(block, ('dom', 'ref'), pairs)  5.89 us
    pallas_call x4, Pallas kernels, on_vmem(): pl.pallas_call(body, out_shape=jax.ShapeDtypeStruct((rows, args[0].shape[...  2.55 us
    ppermute x4, waiting for transfers between devices, partner_blocks(): came = lax.ppermute(block, ('dom', 'ref'), pairs)  2.08 us
    unnamed x6, local copies, waits for them, and re-layouts  1.89 us
    div x1, other arithmetic, on_device(): return (own_rows, (own_rows - start_rows) / step_size)  1.34 us
  transfers between devices with their start and end apart: 9, of which 5 were waited for; matrix products, arithmetic and copies ran while one was open for 0% of the time, Pallas kernels for 4%

profile of v1, /device:TPU:0, one launch (start us, length us, event | category | flops | bytes accessed | tf_op | source)
XLA Modules:
  0.0 35.6 jit_solution(10161518215062739379)
XLA Ops:
  0.6 0.7 %collective-permute-start = (f32[128,128]{1,0:T(8,128)}, f32[128,128]{1,0:T(8,128)S(1)}, u32[]{:S(2)}, u32[]{:S(2)}) collective-permute-start(f32[128,128]{1,0:T(8,128)} %block_ref.3), channel_id=1, source_target_pairs={{1,17},{2,10},{3,27},{5,21},{6,14},{7,31},{9,25},{10,2},{11,19},{1... | collective-permute-start | bytes 196616 | tf_op jit(solution)/shard_map/ppermute | solution.py:108
  1.3 3.0 %collective-permute-start.1 = (f32[128,128]{1,0:T(8,128)}, f32[128,128]{1,0:T(8,128)S(1)}, u32[]{:S(2)}, u32[]{:S(2)}) collective-permute-start(f32[128,128]{1,0:T(8,128)} %block_ref.3), channel_id=1, source_target_pairs={{0,4},{1,21},{2,14},{3,31},{4,0},{5,17},{6,10},{7,27},{8,12},{9,29... | collective-permute-start | bytes 196616 | tf_op jit(solution)/shard_map/ppermute | solution.py:108
  4.3 0.0 copy-start
  4.3 1.0 %copy-done = f32[1024,128]{1,0:T(8,128)S(1)} copy-done((f32[1024,128]{1,0:T(8,128)S(1)}, f32[1024,128]{1,0:T(8,128)}, u32[]{:S(2)}) %copy-start) | copy-done | bytes 524312
  5.3 0.0 copy-start.2
  5.3 0.8 %copy-done.2 = f32[128,128]{1,0:T(8,128)S(1)} copy-done((f32[128,128]{1,0:T(8,128)S(1)}, f32[128,128]{1,0:T(8,128)}, u32[]{:S(2)}) %copy-start.2) | copy-done | bytes 65560
  6.2 0.7 %shard_map.41.first_ref = f32[128,128]{1,0:T(8,128)S(1)} custom-call(f32[128,128]{1,0:T(8,128)S(1)} %copy-done.2, f32[1024,128]{1,0:T(8,128)S(1)} %copy-done), custom_call_target="tpu_custom_call" | custom-call | flops 134217728 | bytes 589824 | tf_op jit(solution)/shard_map/pallas_call | solution.py:73
  6.9 0.0 copy-start.1
  6.9 0.0 collective-permute-done
  6.9 0.0 collective-permute-done.1.refs_1_
  6.9 0.6 %shard_map.42 = f32[128,128]{1,0:T(8,128)S(1)} custom-call(f32[128,128]{1,0:T(8,128)S(1)} %copy-done.2, f32[128,128]{1,0:T(8,128)S(1)} %shard_map.41.first_ref, f32[128,128]{1,0:T(8,128)S(1)} %broadcast_select_fusion.1.refs_0_, f32[128,128]{1,0:T(8,128)S(1)} %collective-permute-done.1.refs_1_), custom_call_target="tpu_custom_call" | custom-call | flops 16777216 | bytes 262144 | tf_op jit(solution)/shard_map/pallas_call | solution.py:73
  7.5 4.5 %collective-permute-start.2 = (f32[128,128]{1,0:T(8,128)S(1)}, f32[128,128]{1,0:T(8,128)S(1)}, u32[]{:S(2)}, u32[]{:S(2)}) collective-permute-start(f32[128,128]{1,0:T(8,128)S(1)} %shard_map.42), channel_id=1, source_target_pairs={{0,1},{1,0},{2,3},{3,2},{4,5},{5,4},{6,7},{7,6},{8,9},{9,8},{10,11... | collective-permute-start | bytes 196616 | tf_op jit(solution)/shard_map/ppermute | solution.py:89
  12.0 0.9 %collective-permute-done.2 = f32[128,128]{1,0:T(8,128)S(1)} collective-permute-done((f32[128,128]{1,0:T(8,128)S(1)}, f32[128,128]{1,0:T(8,128)S(1)}, u32[]{:S(2)}, u32[]{:S(2)}) %collective-permute-start.2) | collective-permute-done | bytes 65568 | tf_op jit(solution)/shard_map/ppermute | solution.py:89
  12.9 3.8 %collective-permute-start.3 = (f32[128,128]{1,0:T(8,128)S(1)}, f32[128,128]{1,0:T(8,128)S(1)}, u32[]{:S(2)}, u32[]{:S(2)}) collective-permute-start(f32[128,128]{1,0:T(8,128)S(1)} %add.29), channel_id=1, source_target_pairs={{0,2},{1,3},{2,0},{3,1},{4,6},{5,7},{6,4},{7,5},{8,10},{9,11},{10,... | collective-permute-start | bytes 196616 | tf_op jit(solution)/shard_map/ppermute | solution.py:89
  16.7 2.6 %collective-permute-done.3 = f32[128,128]{1,0:T(8,128)S(1)} collective-permute-done((f32[128,128]{1,0:T(8,128)S(1)}, f32[128,128]{1,0:T(8,128)S(1)}, u32[]{:S(2)}, u32[]{:S(2)}) %collective-permute-start.3) | collective-permute-done | bytes 65568 | tf_op jit(solution)/shard_map/ppermute | solution.py:89
  19.4 0.7 %collective-permute-start.4 = (f32[128,128]{1,0:T(8,128)S(1)}, f32[128,128]{1,0:T(8,128)S(1)}, u32[]{:S(2)}, u32[]{:S(2)}) collective-permute-start(f32[128,128]{1,0:T(8,128)S(1)} %multiply_subtract_fusion.block_ref), channel_id=1, source_target_pairs={{1,17},{2,10},{3,27},{5,21},{6,14},{7,31},{9,25},{10,2},{11,19},{1... | collective-permute-start | bytes 196616 | tf_op jit(solution)/shard_map/ppermute | solution.py:108
  20.1 1.6 %collective-permute-start.5 = (f32[128,128]{1,0:T(8,128)S(1)}, f32[128,128]{1,0:T(8,128)S(1)}, u32[]{:S(2)}, u32[]{:S(2)}) collective-permute-start(f32[128,128]{1,0:T(8,128)S(1)} %multiply_subtract_fusion.block_ref), channel_id=1, source_target_pairs={{0,4},{1,21},{2,14},{3,31},{4,0},{5,17},{6,10},{7,27},{8,12},{9,29... | collective-permute-start | bytes 196616 | tf_op jit(solution)/shard_map/ppermute | solution.py:108
  21.6 0.0 copy-done.1
  21.6 0.7 %shard_map.43.first_ref = f32[128,128]{1,0:T(8,128)S(1)} custom-call(f32[128,128]{1,0:T(8,128)S(1)} %multiply_subtract_fusion.block_ref, f32[1024,128]{1,0:T(8,128)S(1)} %copy-done.1), custom_call_target="tpu_custom_call" | custom-call | flops 134217728 | bytes 589824 | tf_op jit(solution)/shard_map/pallas_call | solution.py:73
  22.3 0.0 collective-permute-done.4
  22.3 2.1 %collective-permute-done.5.refs_1_ = f32[128,128]{1,0:T(8,128)S(1)} collective-permute-done((f32[128,128]{1,0:T(8,128)S(1)}, f32[128,128]{1,0:T(8,128)S(1)}, u32[]{:S(2)}, u32[]{:S(2)}) %collective-permute-start.5) | collective-permute-done | bytes 65568 | tf_op jit(solution)/shard_map/ppermute | solution.py:108
  24.4 0.6 %shard_map.44 = f32[128,128]{1,0:T(8,128)S(1)} custom-call(f32[128,128]{1,0:T(8,128)S(1)} %multiply_subtract_fusion.block_ref, f32[128,128]{1,0:T(8,128)S(1)} %shard_map.43.first_ref, f32[128,128]{1,0:T(8,128)S(1)} %broadcast_select_fusion.refs_0_, f32[128,128]{1,0:T(8,128)S(1)} %collective-permute-done.5.refs_1_), custom_call_target="tpu_custom_call" | custom-call | flops 16777216 | bytes 262144 | tf_op jit(solution)/shard_map/pallas_call | solution.py:73
  25.0 2.4 %collective-permute-start.6 = (f32[32,128]{1,0:T(8,128)S(1)}, f32[32,128]{1,0:T(8,128)S(1)}, u32[]{:S(2)}, u32[]{:S(2)}) collective-permute-start(f32[32,128]{1,0:T(8,128)S(1)} %get-tuple-element.4), channel_id=1, source_target_pairs={{0,1},{1,0},{2,3},{3,2},{4,5},{5,4},{6,7},{7,6},{8,9},{9,8},{10,11... | collective-permute-start | bytes 49160 | tf_op jit(solution)/shard_map/ppermute | solution.py:89
  27.4 3.7 %collective-permute-start.7 = (f32[32,128]{1,0:T(8,128)S(1)}, f32[32,128]{1,0:T(8,128)S(1)}, u32[]{:S(2)}, u32[]{:S(2)}) collective-permute-start(f32[32,128]{1,0:T(8,128)S(1)} %get-tuple-element.6), channel_id=1, source_target_pairs={{0,2},{1,3},{2,0},{3,1},{4,6},{5,7},{6,4},{7,5},{8,10},{9,11},{10,... | collective-permute-start | bytes 49160 | tf_op jit(solution)/shard_map/ppermute | solution.py:89
  31.1 0.1 collective-permute-start.8
  31.1 0.0 collective-permute-done.6
  31.1 1.6 %collective-permute-done.7 = f32[32,128]{1,0:T(8,128)S(1)} collective-permute-done((f32[32,128]{1,0:T(8,128)S(1)}, f32[32,128]{1,0:T(8,128)S(1)}, u32[]{:S(2)}, u32[]{:S(2)}) %collective-permute-start.7) | collective-permute-done | bytes 16416 | tf_op jit(solution)/shard_map/ppermute | solution.py:89
  32.8 1.4 %collective-permute-done.8 = f32[32,128]{1,0:T(8,128)S(1)} collective-permute-done((f32[32,128]{1,0:T(8,128)S(1)}, f32[32,128]{1,0:T(8,128)S(1)}, u32[]{:S(2)}, u32[]{:S(2)}) %collective-permute-start.8) | collective-permute-done | bytes 16416 | tf_op jit(solution)/shard_map/ppermute | solution.py:89
  34.2 1.3 %subtract_multiply_fusion = (f32[32,128]{1,0:T(8,128)}, f32[32,128]{1,0:T(8,128)}) fusion(f32[128,128]{1,0:T(8,128)} %block_ref.3, s32[]{:T(128)S(6)} %select_n.28, f32[32,128]{1,0:T(8,128)S(1)} %collective-permute-done.8, f32[32,128]{1,0:T(8,128)S(1)} %collective-permute-done.7, f32[32,128]{1,0:T(8,128)S(1)} %collective-permute-done.6, ...), kind=kLoop, calls=%fused_computation.3 | loop fusion | flops 28672 | bytes 131076 | tf_op jit(solution)/shard_map/div | solution.py:147
  (5 shorter events, 0.1 us)
Async XLA Ops:
  0.6 6.2 %collective-permute-start = (f32[128,128]{1,0:T(8,128)}, f32[128,128]{1,0:T(8,128)S(1)}, u32[]{:S(2)}, u32[]{:S(2)}) collective-permute-start(f32[128,128]{1,0:T(8,128)} %block_ref.3), channel_id=1, source_target_pairs={{1,17},{2,10},{3,27},{5,21},{6,14},{7,31},{9,25},{10,2},{11,19},{1... | collective-permute-start | bytes 196616 | tf_op jit(solution)/shard_map/ppermute | solution.py:108
  1.3 5.6 %collective-permute-start.1 = (f32[128,128]{1,0:T(8,128)}, f32[128,128]{1,0:T(8,128)S(1)}, u32[]{:S(2)}, u32[]{:S(2)}) collective-permute-start(f32[128,128]{1,0:T(8,128)} %block_ref.3), channel_id=1, source_target_pairs={{0,4},{1,21},{2,14},{3,31},{4,0},{5,17},{6,10},{7,27},{8,12},{9,29... | collective-permute-start | bytes 196616 | tf_op jit(solution)/shard_map/ppermute | solution.py:108
  4.3 1.0 %copy-start = (f32[1024,128]{1,0:T(8,128)S(1)}, f32[1024,128]{1,0:T(8,128)}, u32[]{:S(2)}) copy-start(f32[1024,128]{1,0:T(8,128)} %others_ref.3) | copy-start | bytes 1572868
  5.3 0.8 %copy-start.2 = (f32[128,128]{1,0:T(8,128)S(1)}, f32[128,128]{1,0:T(8,128)}, u32[]{:S(2)}) copy-start(f32[128,128]{1,0:T(8,128)} %block_ref.3) | copy-start | bytes 196612
  6.9 14.7 %copy-start.1 = (f32[1024,128]{1,0:T(8,128)S(1)}, f32[1024,128]{1,0:T(8,128)}, u32[]{:S(2)}) copy-start(f32[1024,128]{1,0:T(8,128)} %others_ref.3) | copy-start | bytes 1572868
  7.5 5.4 %collective-permute-start.2 = (f32[128,128]{1,0:T(8,128)S(1)}, f32[128,128]{1,0:T(8,128)S(1)}, u32[]{:S(2)}, u32[]{:S(2)}) collective-permute-start(f32[128,128]{1,0:T(8,128)S(1)} %shard_map.42), channel_id=1, source_target_pairs={{0,1},{1,0},{2,3},{3,2},{4,5},{5,4},{6,7},{7,6},{8,9},{9,8},{10,11... | collective-permute-start | bytes 196616 | tf_op jit(solution)/shard_map/ppermute | solution.py:89
  12.9 6.4 %collective-permute-start.3 = (f32[128,128]{1,0:T(8,128)S(1)}, f32[128,128]{1,0:T(8,128)S(1)}, u32[]{:S(2)}, u32[]{:S(2)}) collective-permute-start(f32[128,128]{1,0:T(8,128)S(1)} %add.29), channel_id=1, source_target_pairs={{0,2},{1,3},{2,0},{3,1},{4,6},{5,7},{6,4},{7,5},{8,10},{9,11},{10,... | collective-permute-start | bytes 196616 | tf_op jit(solution)/shard_map/ppermute | solution.py:89
  19.4 2.9 %collective-permute-start.4 = (f32[128,128]{1,0:T(8,128)S(1)}, f32[128,128]{1,0:T(8,128)S(1)}, u32[]{:S(2)}, u32[]{:S(2)}) collective-permute-start(f32[128,128]{1,0:T(8,128)S(1)} %multiply_subtract_fusion.block_ref), channel_id=1, source_target_pairs={{1,17},{2,10},{3,27},{5,21},{6,14},{7,31},{9,25},{10,2},{11,19},{1... | collective-permute-start | bytes 196616 | tf_op jit(solution)/shard_map/ppermute | solution.py:108
  20.1 4.3 %collective-permute-start.5 = (f32[128,128]{1,0:T(8,128)S(1)}, f32[128,128]{1,0:T(8,128)S(1)}, u32[]{:S(2)}, u32[]{:S(2)}) collective-permute-start(f32[128,128]{1,0:T(8,128)S(1)} %multiply_subtract_fusion.block_ref), channel_id=1, source_target_pairs={{0,4},{1,21},{2,14},{3,31},{4,0},{5,17},{6,10},{7,27},{8,12},{9,29... | collective-permute-start | bytes 196616 | tf_op jit(solution)/shard_map/ppermute | solution.py:108
  25.0 6.1 %collective-permute-start.6 = (f32[32,128]{1,0:T(8,128)S(1)}, f32[32,128]{1,0:T(8,128)S(1)}, u32[]{:S(2)}, u32[]{:S(2)}) collective-permute-start(f32[32,128]{1,0:T(8,128)S(1)} %get-tuple-element.4), channel_id=1, source_target_pairs={{0,1},{1,0},{2,3},{3,2},{4,5},{5,4},{6,7},{7,6},{8,9},{9,8},{10,11... | collective-permute-start | bytes 49160 | tf_op jit(solution)/shard_map/ppermute | solution.py:89
  27.4 5.4 %collective-permute-start.7 = (f32[32,128]{1,0:T(8,128)S(1)}, f32[32,128]{1,0:T(8,128)S(1)}, u32[]{:S(2)}, u32[]{:S(2)}) collective-permute-start(f32[32,128]{1,0:T(8,128)S(1)} %get-tuple-element.6), channel_id=1, source_target_pairs={{0,2},{1,3},{2,0},{3,1},{4,6},{5,7},{6,4},{7,5},{8,10},{9,11},{10,... | collective-permute-start | bytes 49160 | tf_op jit(solution)/shard_map/ppermute | solution.py:89
  31.1 3.2 %collective-permute-start.8 = (f32[32,128]{1,0:T(8,128)S(1)}, f32[32,128]{1,0:T(8,128)S(1)}, u32[]{:S(2)}, u32[]{:S(2)}) collective-permute-start(f32[32,128]{1,0:T(8,128)S(1)} %get-tuple-element.5), channel_id=1, source_target_pairs={{0,3},{1,2},{2,1},{3,0},{4,7},{5,6},{6,5},{7,4},{8,11},{9,10},{10,... | collective-permute-start | bytes 49160 | tf_op jit(solution)/shard_map/ppermute | solution.py:89

commit v2 on v1

--- a/solution.py
+++ b/solution.py
@@ -44,42 +44,51 @@
     return pulled[:, :width] + pulled[:, width:], jnp.sum(weights, axis=1, keepdims=True)
 
 
-def all_terms(block, others_ref):
+def tiles_of(others):
+    count = sum(other.shape[0] for other in others)
+    if count <= TILE:
+        return [jnp.concatenate([other[...] for other in others], axis=0)]
+    return [
+        other[pl.ds(start, min(TILE, other.shape[0])), :]
+        for other in others
+        for start in range(0, other.shape[0], TILE)
+    ]
+
+
+def all_terms(block, others):
     left = left_operand(block)
     left_square = jnp.sum(block * block, axis=1, keepdims=True) * (-0.5 * LOG2E)
-    count = others_ref.shape[0]
-    tile = min(TILE, count)
     pulled = jnp.zeros(block.shape, jnp.float32)
     summed = jnp.zeros((block.shape[0], 1), jnp.float32)
-    for start in range(0, count, tile):
-        more = kernel_terms(left, left_square, others_ref[pl.ds(start, tile), :])
+    for tile in tiles_of(others):
+        more = kernel_terms(left, left_square, tile)
         pulled, summed = pulled + more[0], summed + more[1]
     return pulled - summed * block
 
 
-def references_kernel(count_r, block_ref, others_ref, out_ref):
-    out_ref[...] = all_terms(block_ref[...], others_ref) * (-1.0 / count_r)
+def references_kernel(count_r, block_ref, others_ref, out_ref, *own_refs):
+    out_ref[...] = all_terms(block_ref[...], [others_ref]) * (-1.0 / count_r)
+    for own_ref in own_refs:
+        rows = own_ref.shape[0]
+        own_ref[...] = block_ref[pl.ds(pl.multiple_of(lax.axis_index("ref") * rows, rows), rows), :]
 
 
 def partners_kernel(count_p, block_ref, first_ref, *refs):
     other_refs, out_ref = refs[:-1], refs[-1]
-    total = first_ref[...]
-    for other in other_refs:
-        total += all_terms(block_ref[...], other) * (1.0 / count_p)
-    out_ref[...] = total
+    out_ref[...] = first_ref[...] + all_terms(block_ref[...], other_refs) * (1.0 / count_p)
 
 
 def on_vmem(body, rows, *args):
     return pl.pallas_call(
         body,
-        out_shape=jax.ShapeDtypeStruct((rows, args[0].shape[1]), jnp.float32),
+        out_shape=[jax.ShapeDtypeStruct((r, args[0].shape[1]), jnp.float32) for r in rows],
         in_specs=[pl.BlockSpec(memory_space=pltpu.VMEM)] * len(args),
-        out_specs=pl.BlockSpec(memory_space=pltpu.VMEM),
+        out_specs=[pl.BlockSpec(memory_space=pltpu.VMEM)] * len(rows),
         compiler_params=pltpu.CompilerParams(vmem_limit_bytes=40 << 20),
         cost_estimate=pl.CostEstimate(
-            flops=8 * rows * args[1].shape[0] * args[0].shape[1],
+            flops=8 * rows[0] * args[1].shape[0] * args[0].shape[1],
             bytes_accessed=4 * sum(a.size for a in args),
-            transcendentals=rows * args[1].shape[0],
+            transcendentals=rows[0] * args[1].shape[0],
         ),
     )(*args)
 
@@ -91,8 +100,10 @@
 
 def offsets_of(n_dom, n_ref):
     share = n_dom // n_ref
-    order = [0, 2, 1, 3] if n_ref == 4 else list(range(n_ref))
-    return [[order[r] * share + i for i in range(share)] for r in range(n_ref)]
+    return [
+        [i * n_ref + (r if i % 2 == 0 else n_ref - 1 - r) for i in reversed(range(share))]
+        for r in range(n_ref)
+    ]
 
 
 def partner_blocks(block, n_dom, n_ref):
@@ -103,13 +114,8 @@
             (d * n_ref + r, (d ^ offsets[r][i]) * n_ref + r)
             for d in range(n_dom)
             for r in range(n_ref)
-            if offsets[r][i]
         ]
-        came = lax.ppermute(block, ("dom", "ref"), pairs)
-        own = [r for r in range(n_ref) if not offsets[r][i]]
-        if own:
-            came = jnp.where(lax.axis_index("ref") == own[0], block, came)
-        blocks.append(came)
+        blocks.append(lax.ppermute(block, ("dom", "ref"), pairs))
     return blocks
 
 
@@ -121,15 +127,19 @@
     count_p = block_rows * n_dom
     count_r = references.shape[0] * n_ref
     place = lax.axis_index("ref")
-    start_rows = lax.dynamic_slice_in_dim(particles, place * rows, rows, 0)
     block = particles
     for step in range(STEPS):
         partners = partner_blocks(block, n_dom, n_ref)
-        partial_value = on_vmem(
-            functools.partial(references_kernel, count_r), block_rows, block, references
+        partial_value, *own = on_vmem(
+            functools.partial(references_kernel, count_r),
+            [block_rows, rows],
+            block,
+            references,
         )
-        partial_value = on_vmem(
-            functools.partial(partners_kernel, count_p), block_rows, block, partial_value, *partners
+        if step == 0:
+            start_rows = own[0]
+        (partial_value,) = on_vmem(
+            functools.partial(partners_kernel, count_p), [block_rows], block, partial_value, *partners
         )
         if step + 1 < STEPS:
             offset = 1
@@ -142,8 +152,7 @@
             for offset in range(1, n_ref):
                 chunk = lax.dynamic_slice_in_dim(partial_value, (place ^ offset) * rows, rows, 0)
                 total = total + exchange(chunk, "ref", offset)
-            own_rows = lax.dynamic_slice_in_dim(block, place * rows, rows, 0)
-            own_rows = own_rows - step_size * total
+            own_rows = own[0] - step_size * total
     return (own_rows, (own_rows - start_rows) / step_size)
 
 

time: 35.8 us -> 30 us (0.84)
  starting transfers between devices: 20.3 us -> 15.5 us
  other arithmetic: 1.38 us -> 0.64 us
  Pallas kernels: 2.55 us -> 2.17 us
    ppermute x5, starting transfers between devices: 14.4 us -> 5.09 us  [exchange(): return lax.ppermute(values, axis, [(i, i ^ offset) for i in range(size)])]
    ppermute x4, starting transfers between devices: 5.89 us -> 10.4 us  [partner_blocks(): blocks.append(lax.ppermute(block, ('dom', 'ref'), pairs))]
    ppermute x4, waiting for transfers between devices: 2.08 us -> 3.44 us  [partner_blocks(): blocks.append(lax.ppermute(block, ('dom', 'ref'), pairs))]
    ppermute x5, waiting for transfers between devices: 6.61 us -> 5.37 us  [exchange(): return lax.ppermute(values, axis, [(i, i ^ offset) for i in range(size)])]
    div x1, other arithmetic: 1.34 us -> 0.62 us  [on_device(): return (own_rows, (own_rows - start_rows) / step_size)]
    pallas_call x4, Pallas kernels: 2.55 us -> 2.17 us  [on_vmem(): pl.pallas_call(body, out_shape=[jax.ShapeDtypeStruct((r, args[0].shape[1]...]
where the time goes in v2:
time: 30 us; the launch traced here: 29.8 us
  starting transfers between devices  15.5 us (52%)
  waiting for transfers between devices  8.8 us (29%)
  Pallas kernels  2.17 us (7%)
  local copies, waits for them, and re-layouts  1.9 us (6%)
  between operations  0.75 us (2%)
  other arithmetic  0.64 us (2%)
    ppermute x4, starting transfers between devices, partner_blocks(): blocks.append(lax.ppermute(block, ('dom', 'ref'), pairs))  10.4 us
    ppermute x5, waiting for transfers between devices, exchange(): return lax.ppermute(values, axis, [(i, i ^ offset) for i in range(size)])  5.37 us
    ppermute x5, starting transfers between devices, exchange(): return lax.ppermute(values, axis, [(i, i ^ offset) for i in range(size)])  5.09 us
    ppermute x4, waiting for transfers between devices, partner_blocks(): blocks.append(lax.ppermute(block, ('dom', 'ref'), pairs))  3.44 us
    pallas_call x4, Pallas kernels, on_vmem(): pl.pallas_call(body, out_shape=[jax.ShapeDtypeStruct((r, args[0].shape[1]...  2.17 us
    unnamed x6, local copies, waits for them, and re-layouts  1.89 us
    div x1, other arithmetic, on_device(): return (own_rows, (own_rows - start_rows) / step_size)  0.62 us
  transfers between devices with their start and end apart: 9, of which 5 were waited for; matrix products, arithmetic and copies ran while one was open for 0% of the time, Pallas kernels for 4%

profile of v2, /device:TPU:0, one launch (start us, length us, event | category | flops | bytes accessed | tf_op | source)
XLA Modules:
  0.0 29.8 jit_solution(11574439224865277785)
XLA Ops:
  0.6 6.0 %collective-permute-start = (f32[128,128]{1,0:T(8,128)}, f32[128,128]{1,0:T(8,128)S(1)}, u32[]{:S(2)}, u32[]{:S(2)}) collective-permute-start(f32[128,128]{1,0:T(8,128)} %block_ref.3), channel_id=1, source_target_pairs={{0,28},{1,25},{2,22},{3,19},{4,24},{5,29},{6,18},{7,23},{8,20},{9,... | collective-permute-start | bytes 196616 | tf_op jit(solution)/shard_map/ppermute | solution.py:118
  6.7 1.5 %collective-permute-start.1 = (f32[128,128]{1,0:T(8,128)}, f32[128,128]{1,0:T(8,128)S(1)}, u32[]{:S(2)}, u32[]{:S(2)}) collective-permute-start(f32[128,128]{1,0:T(8,128)} %block_ref.3), channel_id=1, source_target_pairs={{0,0},{1,5},{2,10},{3,15},{4,4},{5,1},{6,14},{7,11},{8,8},{9,13},{... | collective-permute-start | bytes 196616 | tf_op jit(solution)/shard_map/ppermute | solution.py:118
  8.2 0.0 copy-start
  8.2 1.0 %copy-done = f32[1024,128]{1,0:T(8,128)S(1)} copy-done((f32[1024,128]{1,0:T(8,128)S(1)}, f32[1024,128]{1,0:T(8,128)}, u32[]{:S(2)}) %copy-start) | copy-done | bytes 524312
  9.2 0.0 copy-start.2
  9.2 0.8 %copy-done.2 = f32[128,128]{1,0:T(8,128)S(1)} copy-done((f32[128,128]{1,0:T(8,128)S(1)}, f32[128,128]{1,0:T(8,128)}, u32[]{:S(2)}) %copy-start.2) | copy-done | bytes 65560
  10.0 0.7 %shard_map.41 = (f32[128,128]{1,0:T(8,128)S(1)}, f32[32,128]{1,0:T(8,128)S(1)}) custom-call(f32[128,128]{1,0:T(8,128)S(1)} %copy-done.2, f32[1024,128]{1,0:T(8,128)S(1)} %copy-done), custom_call_target="tpu_custom_call" | custom-call | flops 134217728 | bytes 589824 | tf_op jit(solution)/shard_map/pallas_call | solution.py:82
  10.7 0.0 copy-start.1
  10.7 0.0 collective-permute-done.refs_0_
  10.7 0.0 collective-permute-done.1.refs_1_
  10.7 0.4 %shard_map.42 = f32[128,128]{1,0:T(8,128)S(1)} custom-call(f32[128,128]{1,0:T(8,128)S(1)} %copy-done.2, f32[128,128]{1,0:T(8,128)S(1)} %get-tuple-element.6.first_ref, f32[128,128]{1,0:T(8,128)S(1)} %collective-permute-done.refs_0_, f32[128,128]{1,0:T(8,128)S(1)} %collective-permute-done.1.refs_1_), custom_call_target="tpu_custom_call" | custom-call | flops 16777216 | bytes 262144 | tf_op jit(solution)/shard_map/pallas_call | solution.py:82
  11.2 0.3 %collective-permute-start.2 = (f32[128,128]{1,0:T(8,128)S(1)}, f32[128,128]{1,0:T(8,128)S(1)}, u32[]{:S(2)}, u32[]{:S(2)}) collective-permute-start(f32[128,128]{1,0:T(8,128)S(1)} %shard_map.42), channel_id=1, source_target_pairs={{0,1},{1,0},{2,3},{3,2},{4,5},{5,4},{6,7},{7,6},{8,9},{9,8},{10,11... | collective-permute-start | bytes 196616 | tf_op jit(solution)/shard_map/ppermute | solution.py:98
  11.5 1.0 %collective-permute-done.2 = f32[128,128]{1,0:T(8,128)S(1)} collective-permute-done((f32[128,128]{1,0:T(8,128)S(1)}, f32[128,128]{1,0:T(8,128)S(1)}, u32[]{:S(2)}, u32[]{:S(2)}) %collective-permute-start.2) | collective-permute-done | bytes 65568 | tf_op jit(solution)/shard_map/ppermute | solution.py:98
  12.5 2.9 %collective-permute-start.3 = (f32[128,128]{1,0:T(8,128)S(1)}, f32[128,128]{1,0:T(8,128)S(1)}, u32[]{:S(2)}, u32[]{:S(2)}) collective-permute-start(f32[128,128]{1,0:T(8,128)S(1)} %add.27), channel_id=1, source_target_pairs={{0,2},{1,3},{2,0},{3,1},{4,6},{5,7},{6,4},{7,5},{8,10},{9,11},{10,... | collective-permute-start | bytes 196616 | tf_op jit(solution)/shard_map/ppermute | solution.py:98
  15.4 2.4 %collective-permute-done.3 = f32[128,128]{1,0:T(8,128)S(1)} collective-permute-done((f32[128,128]{1,0:T(8,128)S(1)}, f32[128,128]{1,0:T(8,128)S(1)}, u32[]{:S(2)}, u32[]{:S(2)}) %collective-permute-start.3) | collective-permute-done | bytes 65568 | tf_op jit(solution)/shard_map/ppermute | solution.py:98
  17.8 2.2 %collective-permute-start.4 = (f32[128,128]{1,0:T(8,128)S(1)}, f32[128,128]{1,0:T(8,128)S(1)}, u32[]{:S(2)}, u32[]{:S(2)}) collective-permute-start(f32[128,128]{1,0:T(8,128)S(1)} %multiply_subtract_fusion.block_ref), channel_id=1, source_target_pairs={{0,28},{1,25},{2,22},{3,19},{4,24},{5,29},{6,18},{7,23},{8,20},{9,... | collective-permute-start | bytes 196616 | tf_op jit(solution)/shard_map/ppermute | solution.py:118
  20.0 0.7 %collective-permute-start.5 = (f32[128,128]{1,0:T(8,128)S(1)}, f32[128,128]{1,0:T(8,128)S(1)}, u32[]{:S(2)}, u32[]{:S(2)}) collective-permute-start(f32[128,128]{1,0:T(8,128)S(1)} %multiply_subtract_fusion.block_ref), channel_id=1, source_target_pairs={{0,0},{1,5},{2,10},{3,15},{4,4},{5,1},{6,14},{7,11},{8,8},{9,13},{... | collective-permute-start | bytes 196616 | tf_op jit(solution)/shard_map/ppermute | solution.py:118
  20.7 0.0 copy-done.1
  20.7 0.7 %shard_map.43 = (f32[128,128]{1,0:T(8,128)S(1)}, f32[32,128]{1,0:T(8,128)S(1)}) custom-call(f32[128,128]{1,0:T(8,128)S(1)} %multiply_subtract_fusion.block_ref, f32[1024,128]{1,0:T(8,128)S(1)} %copy-done.1), custom_call_target="tpu_custom_call" | custom-call | flops 134217728 | bytes 589824 | tf_op jit(solution)/shard_map/pallas_call | solution.py:82
  21.4 3.4 %collective-permute-done.4.refs_0_ = f32[128,128]{1,0:T(8,128)S(1)} collective-permute-done((f32[128,128]{1,0:T(8,128)S(1)}, f32[128,128]{1,0:T(8,128)S(1)}, u32[]{:S(2)}, u32[]{:S(2)}) %collective-permute-start.4) | collective-permute-done | bytes 65568 | tf_op jit(solution)/shard_map/ppermute | solution.py:118
  24.8 0.0 collective-permute-done.5.refs_1_
  24.8 0.4 %shard_map.44 = f32[128,128]{1,0:T(8,128)S(1)} custom-call(f32[128,128]{1,0:T(8,128)S(1)} %multiply_subtract_fusion.block_ref, f32[128,128]{1,0:T(8,128)S(1)} %get-tuple-element.8.first_ref, f32[128,128]{1,0:T(8,128)S(1)} %collective-permute-done.4.refs_0_, f32[128,128]{1,0:T(8,128)S(1)} %collective-permute-done.5.refs_1_), custom_call_target="tpu_custom_call" | custom-call | flops 16777216 | bytes 262144 | tf_op jit(solution)/shard_map/pallas_call | solution.py:82
  25.3 0.1 collective-permute-start.8
  25.3 1.6 %collective-permute-start.7 = (f32[32,128]{1,0:T(8,128)S(1)}, f32[32,128]{1,0:T(8,128)S(1)}, u32[]{:S(2)}, u32[]{:S(2)}) collective-permute-start(f32[32,128]{1,0:T(8,128)S(1)} %get-tuple-element.14), channel_id=1, source_target_pairs={{0,2},{1,3},{2,0},{3,1},{4,6},{5,7},{6,4},{7,5},{8,10},{9,11},{10,... | collective-permute-start | bytes 49160 | tf_op jit(solution)/shard_map/ppermute | solution.py:98
  27.0 0.2 collective-permute-start.6
  27.2 1.4 %collective-permute-done.8 = f32[32,128]{1,0:T(8,128)S(1)} collective-permute-done((f32[32,128]{1,0:T(8,128)S(1)}, f32[32,128]{1,0:T(8,128)S(1)}, u32[]{:S(2)}, u32[]{:S(2)}) %collective-permute-start.8) | collective-permute-done | bytes 16416 | tf_op jit(solution)/shard_map/ppermute | solution.py:98
  28.5 0.6 %collective-permute-done.7 = f32[32,128]{1,0:T(8,128)S(1)} collective-permute-done((f32[32,128]{1,0:T(8,128)S(1)}, f32[32,128]{1,0:T(8,128)S(1)}, u32[]{:S(2)}, u32[]{:S(2)}) %collective-permute-start.7) | collective-permute-done | bytes 16416 | tf_op jit(solution)/shard_map/ppermute | solution.py:98
  29.1 0.0 collective-permute-done.6
  29.1 0.6 %subtract_multiply_fusion = (f32[32,128]{1,0:T(8,128)}, f32[32,128]{1,0:T(8,128)}) fusion(f32[32,128]{1,0:T(8,128)S(1)} %get-tuple-element.9, f32[32,128]{1,0:T(8,128)S(1)} %get-tuple-element.7, f32[32,128]{1,0:T(8,128)S(1)} %collective-permute-done.8, f32[32,128]{1,0:T(8,128)S(1)} %collective-permute-done.7, f32[32,128]{1,0:T(8,128)S(1)} %collective-permute-done.6, ...), kind=kLoop, calls=%fused_computation.1 | loop fusion | flops 28672 | bytes 131076 | tf_op jit(solution)/shard_map/div | solution.py:156
  (3 shorter events, 0.0 us)
Async XLA Ops:
  0.6 10.1 %collective-permute-start = (f32[128,128]{1,0:T(8,128)}, f32[128,128]{1,0:T(8,128)S(1)}, u32[]{:S(2)}, u32[]{:S(2)}) collective-permute-start(f32[128,128]{1,0:T(8,128)} %block_ref.3), channel_id=1, source_target_pairs={{0,28},{1,25},{2,22},{3,19},{4,24},{5,29},{6,18},{7,23},{8,20},{9,... | collective-permute-start | bytes 196616 | tf_op jit(solution)/shard_map/ppermute | solution.py:118
  6.7 4.1 %collective-permute-start.1 = (f32[128,128]{1,0:T(8,128)}, f32[128,128]{1,0:T(8,128)S(1)}, u32[]{:S(2)}, u32[]{:S(2)}) collective-permute-start(f32[128,128]{1,0:T(8,128)} %block_ref.3), channel_id=1, source_target_pairs={{0,0},{1,5},{2,10},{3,15},{4,4},{5,1},{6,14},{7,11},{8,8},{9,13},{... | collective-permute-start | bytes 196616 | tf_op jit(solution)/shard_map/ppermute | solution.py:118
  8.2 1.0 %copy-start = (f32[1024,128]{1,0:T(8,128)S(1)}, f32[1024,128]{1,0:T(8,128)}, u32[]{:S(2)}) copy-start(f32[1024,128]{1,0:T(8,128)} %others_ref.3) | copy-start | bytes 1572868
  9.2 0.8 %copy-start.2 = (f32[128,128]{1,0:T(8,128)S(1)}, f32[128,128]{1,0:T(8,128)}, u32[]{:S(2)}) copy-start(f32[128,128]{1,0:T(8,128)} %block_ref.3) | copy-start | bytes 196612
  10.7 10.0 %copy-start.1 = (f32[1024,128]{1,0:T(8,128)S(1)}, f32[1024,128]{1,0:T(8,128)}, u32[]{:S(2)}) copy-start(f32[1024,128]{1,0:T(8,128)} %others_ref.3) | copy-start | bytes 1572868
  11.2 1.3 %collective-permute-start.2 = (f32[128,128]{1,0:T(8,128)S(1)}, f32[128,128]{1,0:T(8,128)S(1)}, u32[]{:S(2)}, u32[]{:S(2)}) collective-permute-start(f32[128,128]{1,0:T(8,128)S(1)} %shard_map.42), channel_id=1, source_target_pairs={{0,1},{1,0},{2,3},{3,2},{4,5},{5,4},{6,7},{7,6},{8,9},{9,8},{10,11... | collective-permute-start | bytes 196616 | tf_op jit(solution)/shard_map/ppermute | solution.py:98
  12.5 5.3 %collective-permute-start.3 = (f32[128,128]{1,0:T(8,128)S(1)}, f32[128,128]{1,0:T(8,128)S(1)}, u32[]{:S(2)}, u32[]{:S(2)}) collective-permute-start(f32[128,128]{1,0:T(8,128)S(1)} %add.27), channel_id=1, source_target_pairs={{0,2},{1,3},{2,0},{3,1},{4,6},{5,7},{6,4},{7,5},{8,10},{9,11},{10,... | collective-permute-start | bytes 196616 | tf_op jit(solution)/shard_map/ppermute | solution.py:98
  17.8 7.0 %collective-permute-start.4 = (f32[128,128]{1,0:T(8,128)S(1)}, f32[128,128]{1,0:T(8,128)S(1)}, u32[]{:S(2)}, u32[]{:S(2)}) collective-permute-start(f32[128,128]{1,0:T(8,128)S(1)} %multiply_subtract_fusion.block_ref), channel_id=1, source_target_pairs={{0,28},{1,25},{2,22},{3,19},{4,24},{5,29},{6,18},{7,23},{8,20},{9,... | collective-permute-start | bytes 196616 | tf_op jit(solution)/shard_map/ppermute | solution.py:118
  20.0 4.8 %collective-permute-start.5 = (f32[128,128]{1,0:T(8,128)S(1)}, f32[128,128]{1,0:T(8,128)S(1)}, u32[]{:S(2)}, u32[]{:S(2)}) collective-permute-start(f32[128,128]{1,0:T(8,128)S(1)} %multiply_subtract_fusion.block_ref), channel_id=1, source_target_pairs={{0,0},{1,5},{2,10},{3,15},{4,4},{5,1},{6,14},{7,11},{8,8},{9,13},{... | collective-permute-start | bytes 196616 | tf_op jit(solution)/shard_map/ppermute | solution.py:118
  25.3 3.3 %collective-permute-start.8 = (f32[32,128]{1,0:T(8,128)S(1)}, f32[32,128]{1,0:T(8,128)S(1)}, u32[]{:S(2)}, u32[]{:S(2)}) collective-permute-start(f32[32,128]{1,0:T(8,128)S(1)} %get-tuple-element.13), channel_id=1, source_target_pairs={{0,3},{1,2},{2,1},{3,0},{4,7},{5,6},{6,5},{7,4},{8,11},{9,10},{10,... | collective-permute-start | bytes 49160 | tf_op jit(solution)/shard_map/ppermute | solution.py:98
  25.3 3.8 %collective-permute-start.7 = (f32[32,128]{1,0:T(8,128)S(1)}, f32[32,128]{1,0:T(8,128)S(1)}, u32[]{:S(2)}, u32[]{:S(2)}) collective-permute-start(f32[32,128]{1,0:T(8,128)S(1)} %get-tuple-element.14), channel_id=1, source_target_pairs={{0,2},{1,3},{2,0},{3,1},{4,6},{5,7},{6,4},{7,5},{8,10},{9,11},{10,... | collective-permute-start | bytes 49160 | tf_op jit(solution)/shard_map/ppermute | solution.py:98
  27.0 2.2 %collective-permute-start.6 = (f32[32,128]{1,0:T(8,128)S(1)}, f32[32,128]{1,0:T(8,128)S(1)}, u32[]{:S(2)}, u32[]{:S(2)}) collective-permute-start(f32[32,128]{1,0:T(8,128)S(1)} %get-tuple-element.12), channel_id=1, source_target_pairs={{0,1},{1,0},{2,3},{3,2},{4,5},{5,4},{6,7},{7,6},{8,9},{9,8},{10,11... | collective-permute-start | bytes 49160 | tf_op jit(solution)/shard_map/ppermute | solution.py:98

commit v3 on v2

v3 whole, which is shorter than its diff:
```python
import functools

import jax
import jax.numpy as jnp
from jax import lax
from jax.experimental import pallas as pl
from jax.experimental.pallas import tpu as pltpu
from jax.sharding import PartitionSpec as P

STEPS = 2


step_size = 0.5
LOG2E = 1.4426950408889634
TILE = 1024
VMEM_BYTES = 48 << 20
OVER_WIDTH = (((1,), (1,)), ((), ()))
IN_VMEM = pl.BlockSpec(memory_space=pltpu.VMEM)


def split(values):
    high = values.astype(jnp.bfloat16)
    return high, (values - high.astype(jnp.float32)).astype(jnp.bfloat16)


def half_square(values):
    return jnp.sum(values * values, axis=1, keepdims=True) * (-0.5 * LOG2E)


def left_operand(block):
    high, low = split(block * LOG2E)
    return jnp.concatenate(
        [jnp.concatenate([high, high], axis=1), jnp.concatenate([low, low], axis=1)], axis=0
    )


def prepare(others):
    return jnp.concatenate(split(others), axis=1), jnp.transpose(half_square(others))


def kernel_terms(left, left_square, right, square):
    rows = left.shape[0] // 2
    width = right.shape[1] // 2
    both = lax.dot_general(left, right, OVER_WIDTH, preferred_element_type=jnp.float32)
    weights = jnp.exp2(both[:rows] + both[rows:] + (left_square + square))
    pulled = jnp.dot(
        jnp.concatenate(split(weights), axis=0), right, preferred_element_type=jnp.float32
    )
    pulled = pulled[:rows] + pulled[rows:]
    return pulled[:, :width] + pulled[:, width:], jnp.sum(weights, axis=1, keepdims=True)


def all_terms(block, pieces):
    left = left_operand(block)
    left_square = half_square(block)
    pulled = jnp.zeros(block.shape, jnp.float32)
    summed = jnp.zeros((block.shape[0], 1), jnp.float32)
    for right, square in pieces:
        count = right.shape[0]
        for start in range(0, count, TILE):
            tile = slice(start, min(start + TILE, count))
            more = kernel_terms(left, left_square, right[tile, :], square[:, tile])
            pulled, summed = pulled + more[0], summed + more[1]
    return pulled - summed * block


def joined(refs):
    return jnp.concatenate([ref[...] for ref in refs], axis=0) if len(refs) > 1 else refs[0][...]


def own_slice(ref, rows):
    return ref[pl.ds(pl.multiple_of(lax.axis_index("ref") * rows, rows), rows), :]


def f32(*shape):
    return jax.ShapeDtypeStruct(shape, jnp.float32)


def exchange(values, axis, offset):
    size = lax.axis_size(axis)
    return lax.ppermute(values, axis, [(i, i ^ offset) for i in range(size)])


def after(values, *earlier):
    return lax.optimization_barrier((values,) + earlier)[0]


def references_kernel(count_r, block_ref, others_ref, out_ref, own_ref):
    block = block_ref[...]
    out_ref[...] = all_terms(block, [prepare(others_ref[...])]) * (-1.0 / count_r)
    own_ref[...] = own_slice(block_ref, own_ref.shape[0])


def partners_kernel(count_p, block_ref, first_ref, *refs):
    other_refs, out_ref = refs[:-1], refs[-1]
    others = prepare(joined(other_refs))
    out_ref[...] = first_ref[...] + all_terms(block_ref[...], [others]) * (1.0 / count_p)


def on_vmem(body, rows, *args):
    return pl.pallas_call(
        body,
        out_shape=[f32(r, args[0].shape[1]) for r in rows],
        in_specs=[IN_VMEM] * len(args),
        out_specs=[IN_VMEM] * len(rows),
        compiler_params=pltpu.CompilerParams(vmem_limit_bytes=VMEM_BYTES),
        cost_estimate=pl.CostEstimate(
            flops=8 * rows[0] * args[1].shape[0] * args[0].shape[1],
            bytes_accessed=4 * sum(a.size for a in args),
            transcendentals=rows[0] * args[1].shape[0],
        ),
    )(*args)


def offsets_of(n_dom, n_ref):
    share = n_dom // n_ref
    return [
        [i * n_ref + (r if i % 2 == 0 else n_ref - 1 - r) for i in reversed(range(share))]
        for r in range(n_ref)
    ]


def partner_blocks(block, n_dom, n_ref):
    offsets = offsets_of(n_dom, n_ref)
    blocks = []
    for i in range(n_dom // n_ref):
        pairs = [
            (d * n_ref + r, (d ^ offsets[r][i]) * n_ref + r)
            for d in range(n_dom)
            for r in range(n_ref)
        ]
        blocks.append(lax.ppermute(block, ("dom", "ref"), pairs))
    return blocks


def exchange_plan(particles, references):
    n_ref = lax.axis_size("ref")
    n_dom = lax.axis_size("dom")
    block_rows = particles.shape[0]
    rows = block_rows // n_ref
    count_p = block_rows * n_dom
    count_r = references.shape[0] * n_ref
    place = lax.axis_index("ref")
    block = particles
    for step in range(STEPS):
        partners = partner_blocks(block, n_dom, n_ref)
        partial_value, own = on_vmem(
            functools.partial(references_kernel, count_r),
            [block_rows, rows],
            block,
            references,
        )
        if step == 0:
            start_rows = own
        (partial_value,) = on_vmem(
            functools.partial(partners_kernel, count_p), [block_rows], block, partial_value, *partners
        )
        if step + 1 < STEPS:
            offset = 1
            while offset < n_ref:
                partial_value = partial_value + exchange(partial_value, "ref", offset)
                offset *= 2
            block = block - step_size * partial_value
        else:
            total = lax.dynamic_slice_in_dim(partial_value, place * rows, rows, 0)
            for offset in range(1, n_ref):
                chunk = lax.dynamic_slice_in_dim(partial_value, (place ^ offset) * rows, rows, 0)
                total = total + exchange(chunk, "ref", offset)
            own_rows = own - step_size * total
    return (own_rows, (own_rows - start_rows) / step_size)


def pull_kernel(scales, counts, has_first, moves, last, own_rows, *refs):
    refs = list(refs)

    def take(count):
        return [refs.pop(0) for _ in range(count)]

    (rows_ref,) = take(1)
    groups = [(take(raw), [tuple(take(2)) for _ in range(pairs)]) for raw, pairs in counts]
    first_refs = take(has_first)
    start_refs = take(last)
    copied_refs = take(own_rows > 0)
    (out_ref,) = take(1)
    rows = rows_ref[...]
    total = first_refs[0][...] if has_first else jnp.zeros(rows.shape, jnp.float32)
    if last:
        (drift_ref,) = take(1)
    if copied_refs:
        copy_ref, own_ref = take(2)
        copy_ref[...] = copied_refs[0][...]
        own_ref[...] = own_slice(copied_refs[0], own_rows)
    for scale, (raw, pairs) in zip(scales, groups):
        pieces = []
        if raw:
            pieces.append(prepare(joined(raw)))
            for ref, value in zip(take(2), pieces[0]):
                ref[...] = value
        pieces += [(right[...], square[...]) for right, square in pairs]
        total += all_terms(rows, pieces) * scale
    if moves:
        total = rows - step_size * total
    out_ref[...] = total
    if last:
        drift_ref[...] = (total - start_refs[0][...]) / step_size


def pull(rows, groups, first=None, moves=False, start=None, copied=None, own_rows=0):
    count, width = rows.shape
    args, outs = [rows], [f32(count, width)]
    if start is not None:
        outs.append(f32(count, width))
    if copied is not None:
        outs += [f32(*copied.shape), f32(own_rows, width)]
    results = len(outs)
    for _, raw, pairs in groups:
        args += list(raw) + [value for pair in pairs for value in pair]
        if raw:
            size = sum(r.shape[0] for r in raw)
            outs += [jax.ShapeDtypeStruct((size, 2 * width), jnp.bfloat16), f32(1, size)]
    args += [value for value in (first, start, copied) if value is not None]
    body = functools.partial(
        pull_kernel,
        [scale for scale, _, _ in groups],
        [(len(raw), len(pairs)) for _, raw, pairs in groups],
        int(first is not None),
        moves,
        int(start is not None),
        own_rows,
    )
    got = pl.pallas_call(
        body,
        out_shape=outs,
        in_specs=[IN_VMEM] * len(args),
        out_specs=[IN_VMEM] * len(outs),
        compiler_params=pltpu.CompilerParams(vmem_limit_bytes=VMEM_BYTES),
        cost_estimate=pl.CostEstimate(flops=1, bytes_accessed=1, transcendentals=0),
    )(*args)
    prepared = [tuple(got[i : i + 2]) for i in range(results, len(got), 2)]
    return list(got[:results]) + prepared


def by_core(values, offsets, n_dom, n_ref):
    pairs = [
        (d * n_ref + r, (d ^ offsets[r % 2]) * n_ref + r) for d in range(n_dom) for r in range(n_ref)
    ]
    return lax.ppermute(values, ("dom", "ref"), pairs)


def gather_plan(particles, references):
    n_ref = lax.axis_size("ref")
    n_dom = lax.axis_size("dom")
    block_rows = particles.shape[0]
    rows = block_rows // n_ref
    for_p = 1.0 / (block_rows * n_dom)
    for_r = -1.0 / (references.shape[0] * n_ref)
    place = lax.axis_index("ref")
    core = place % 2

    across = exchange(references, "ref", 2)
    near = by_core(particles, (2, 1), n_dom, n_ref)
    far = by_core(particles, (6, 7), n_dom, n_ref)
    middle = by_core(particles, (4, 5), n_dom, n_ref)
    mate = exchange(references, "ref", 1)

    near_sum, mate_pair = pull(near, [(for_r, [mate], [])])
    near_sum, own_pair = pull(near, [(for_r, [references], [])], near_sum)
    at_hand = [mate_pair, own_pair]
    relay_pairs = [
        (d * n_ref + r, (d ^ 1) * n_ref + r + 1) for d in range(n_dom) for r in range(0, n_ref, 2)
    ]
    relayed = lax.ppermute(after(near, near_sum), ("dom", "ref"), relay_pairs)
    far_sum, block, start_rows = pull(
        after(far, near_sum), [(for_r, [], at_hand)], copied=particles, own_rows=rows
    )
    middle_sum = pull(after(middle, far_sum), [(for_r, [], at_hand)])[0]
    fourth = jnp.where(core == 0, block, after(relayed, middle_sum))
    fourth_sum = pull(fourth, [(for_r, [], at_hand)])[0]

    held = jnp.concatenate([near, far, middle, fourth])
    held_sum = jnp.concatenate([near_sum, far_sum, middle_sum, fourth_sum])
    held_by_mate = exchange(held, "ref", 1)
    across = after(across, fourth_sum)
    across_mate = exchange(across, "ref", 1)
    held_sum, across_pair = pull(held, [(for_r, [across], [])], held_sum)
    held_sum = pull(held, [(for_p, [held, held_by_mate], [])], held_sum)[0]
    moved, across_mate_pair = pull(held, [(for_r, [across_mate], [])], held_sum, moves=True)

    moved_by_mate = exchange(moved, "ref", 1)
    own_block = jnp.where(core == 0, moved[3 * block_rows :], moved_by_mate[3 * block_rows :])
    own_rows = lax.dynamic_slice_in_dim(own_block, place * rows, rows, 0)
    groups = [
        (for_p, [moved, moved_by_mate], []),
        (for_r, [], at_hand + [across_pair, across_mate_pair]),
    ]
    return tuple(pull(own_rows, groups, moves=True, start=start_rows)[:2])


def on_device(particles, references):
    if (lax.axis_size("dom"), lax.axis_size("ref")) == (8, 4) and STEPS == 2:
        return gather_plan(particles, references)
    return exchange_plan(particles, references)


def solution(mesh):
    placed = (P("dom", None), P("ref", None))
    return jax.shard_map(
        on_device,
        mesh=mesh,
        in_specs=placed,
        out_specs=(P(("dom", "ref"), None), P(("dom", "ref"), None)),
        check_vma=False,
    )
```

time: 30 us -> 26.7 us (0.89)
  Pallas kernels: 2.17 us -> 11.3 us
  waiting for transfers between devices: 8.8 us -> 2.74 us
  starting transfers between devices: 15.5 us -> 11.7 us
  local copies, waits for them, and re-layouts: 1.9 us -> 0.02 us
  other arithmetic: 0.64 us -> 0.05 us
    pallas_call x4 -> x9, Pallas kernels: 2.17 us -> 11.3 us  [pull(): pl.pallas_call(body, out_shape=outs, in_specs=[IN_VMEM] * len(args), out_...]
    ppermute x5, waiting for transfers between devices: 5.37 us -> 1.39 us  [exchange(): return lax.ppermute(values, axis, [(i, i ^ offset) for i in range(size)])]
    ppermute x4, starting transfers between devices: 10.4 us -> 7.38 us  [the longest x3 4.17 us: by_core(): return lax.ppermute(values, ('dom', 'ref'), pairs)]
    ppermute x4, waiting for transfers between devices: 3.44 us -> 1.34 us  [the longest x3 1.34 us: by_core(): return lax.ppermute(values, ('dom', 'ref'), pairs)]
    unnamed x6 -> x4, local copies, waits for them, and re-layouts: 1.89 us -> 0.01 us
    ppermute x5, starting transfers between devices: 5.09 us -> 4.32 us  [exchange(): return lax.ppermute(values, axis, [(i, i ^ offset) for i in range(size)])]
    div x1 -> x0, other arithmetic: 0.62 us -> none  [on_device(): return (own_rows, (own_rows - start_rows) / step_size)]
  transfers between devices with their start and end apart: 9 -> 9, of which waited for: 5 -> 4; matrix products, arithmetic and copies ran while one was open for 0% -> 0% of each run, Pallas kernels for 4% -> 28%
where the time goes in v3:
time: 26.7 us; the launch traced here: 26.5 us
  starting transfers between devices  11.7 us (44%)
  Pallas kernels  11.3 us (42%)
  waiting for transfers between devices  2.74 us (10%)
  between operations  0.76 us (3%)
    pallas_call x9, Pallas kernels, pull(): pl.pallas_call(body, out_shape=outs, in_specs=[IN_VMEM] * len(args), out_...  11.3 us
    ppermute x5, starting transfers between devices, exchange(): return lax.ppermute(values, axis, [(i, i ^ offset) for i in range(size)])  4.32 us
    ppermute x3, starting transfers between devices, by_core(): return lax.ppermute(values, ('dom', 'ref'), pairs)  4.17 us
    ppermute x1, starting transfers between devices, gather_plan(): relayed = lax.ppermute(after(near, near_sum), ('dom', 'ref'), relay_pairs)  3.21 us
    ppermute x5, waiting for transfers between devices, exchange(): return lax.ppermute(values, axis, [(i, i ^ offset) for i in range(size)])  1.39 us
    ppermute x3, waiting for transfers between devices, by_core(): return lax.ppermute(values, ('dom', 'ref'), pairs)  1.34 us
  transfers between devices with their start and end apart: 9, of which 4 were waited for; matrix products, arithmetic and copies ran while one was open for 0% of the time, Pallas kernels for 28%

profile of v3, /device:TPU:0, one launch (start us, length us, event | category | flops | bytes accessed | tf_op | source)
XLA Modules:
  0.0 26.5 jit_solution(10325159182138598566)
XLA Ops:
  0.6 0.0 copy-start
  0.6 0.5 %collective-permute-start.3 = (f32[1024,128]{1,0:T(8,128)}, f32[1024,128]{1,0:T(8,128)S(1)}, u32[]{:S(2)}, u32[]{:S(2)}) collective-permute-start(f32[1024,128]{1,0:T(8,128)} %refs_1_.1), channel_id=1, source_target_pairs={{0,1},{1,0},{2,3},{3,2},{4,5},{5,4},{6,7},{7,6},{8,9},{9,8},{10,11... | collective-permute-start | bytes 1572872 | tf_op jit(solution)/shard_map/ppermute | solution.py:81
  1.2 2.6 %collective-permute-start.5 = (f32[1024,128]{1,0:T(8,128)}, f32[1024,128]{1,0:T(8,128)S(1)}, u32[]{:S(2)}, u32[]{:S(2)}) collective-permute-start(f32[1024,128]{1,0:T(8,128)} %refs_1_.1), channel_id=1, source_target_pairs={{0,2},{1,3},{2,0},{3,1},{4,6},{5,7},{6,4},{7,5},{8,10},{9,11},{10,... | collective-permute-start | bytes 1572872 | tf_op jit(solution)/shard_map/ppermute | solution.py:81
  3.8 1.6 %collective-permute-start = (f32[128,128]{1,0:T(8,128)}, f32[128,128]{1,0:T(8,128)S(1)}, u32[]{:S(2)}, u32[]{:S(2)}) collective-permute-start(f32[128,128]{1,0:T(8,128)} %refs_5_.1), channel_id=1, source_target_pairs={{0,8},{1,5},{2,10},{3,7},{4,12},{5,1},{6,14},{7,3},{8,0},{9,13},{1... | collective-permute-start | bytes 196616 | tf_op jit(solution)/shard_map/ppermute | solution.py:247
  5.3 2.5 %collective-permute-start.1 = (f32[128,128]{1,0:T(8,128)}, f32[128,128]{1,0:T(8,128)S(1)}, u32[]{:S(2)}, u32[]{:S(2)}) collective-permute-start(f32[128,128]{1,0:T(8,128)} %refs_5_.1), channel_id=1, source_target_pairs={{0,24},{1,29},{2,26},{3,31},{4,28},{5,25},{6,30},{7,27},{8,16},{9,... | collective-permute-start | bytes 196616 | tf_op jit(solution)/shard_map/ppermute | solution.py:247
  7.8 0.1 collective-permute-start.2
  7.9 0.3 %collective-permute-done.refs_0_ = f32[128,128]{1,0:T(8,128)S(1)} collective-permute-done((f32[128,128]{1,0:T(8,128)}, f32[128,128]{1,0:T(8,128)S(1)}, u32[]{:S(2)}, u32[]{:S(2)}) %collective-permute-start) | collective-permute-done | bytes 65568 | tf_op jit(solution)/shard_map/ppermute | solution.py:247
  8.2 0.0 collective-permute-done.3.refs_1_
  8.2 0.7 %shard_map.41 = (f32[128,128]{1,0:T(8,128)S(1)}, bf16[1024,256]{1,0:T(8,128)(2,1)S(1)}, f32[1,1024]{1,0:T(1,128)S(1)}) custom-call(f32[128,128]{1,0:T(8,128)S(1)} %collective-permute-done.refs_0_, f32[1024,128]{1,0:T(8,128)S(1)} %collective-permute-done.3.refs_1_), custom_call_target="tpu_custom_call" | custom-call | flops 1 | bytes 1 | tf_op jit(solution)/shard_map/pallas_call | solution.py:231
  8.9 0.0 copy-done
  8.9 0.0 copy-start.1
  8.9 0.7 %shard_map.42 = (f32[128,128]{1,0:T(8,128)S(1)}, bf16[1024,256]{1,0:T(8,128)(2,1)S(1)}, f32[1,1024]{1,0:T(1,128)S(1)}) custom-call(f32[128,128]{1,0:T(8,128)S(1)} %collective-permute-done.refs_0_, f32[1024,128]{1,0:T(8,128)S(1)} %copy-done, f32[128,128]{1,0:T(8,128)S(1)} %get-tuple-element.25.refs_2_), custom_call_target="tpu_custom_call" | custom-call | flops 1 | bytes 1 | tf_op jit(solution)/shard_map/pallas_call | solution.py:231
  9.6 3.2 %collective-permute-start.4 = (f32[128,128]{1,0:T(8,128)S(1)}, f32[128,128]{1,0:T(8,128)S(1)}, u32[]{:S(2)}, u32[]{:S(2)}) collective-permute-start(f32[128,128]{1,0:T(8,128)S(1)} %collective-permute-done.refs_0_), channel_id=1, source_target_pairs={{0,5},{2,7},{4,1},{6,3},{8,13},{10,15},{12,9},{14,11},{16,21},{18,... | collective-permute-start | bytes 196616 | tf_op jit(solution)/shard_map/ppermute | solution.py:272
  12.9 0.0 collective-permute-done.1.refs_0_
  12.9 0.0 copy-done.1
  12.9 0.9 %shard_map.43 = (f32[128,128]{1,0:T(8,128)S(1)}, f32[128,128]{1,0:T(8,128)S(1)}, f32[32,128]{1,0:T(8,128)S(1)}) custom-call(f32[128,128]{1,0:T(8,128)S(1)} %collective-permute-done.1.refs_0_, bf16[1024,256]{1,0:T(8,128)(2,1)S(1)} %get-tuple-element.28.refs_1_.refs_3_, f32[1,1024]{1,0:T(1,128)S(1)} %get-tuple-element.29.refs_2_.refs_4_, ...), custom_call_target="tpu_custom_call" | custom-call | flops 1 | bytes 1 | tf_op jit(solution)/shard_map/pallas_call | solution.py:231
  13.8 1.0 %collective-permute-done.2.refs_0_ = f32[128,128]{1,0:T(8,128)S(1)} collective-permute-done((f32[128,128]{1,0:T(8,128)}, f32[128,128]{1,0:T(8,128)S(1)}, u32[]{:S(2)}, u32[]{:S(2)}) %collective-permute-start.2) | collective-permute-done | bytes 65568 | tf_op jit(solution)/shard_map/ppermute | solution.py:247
  14.8 0.9 %shard_map.44 = f32[128,128]{1,0:T(8,128)S(1)} custom-call(f32[128,128]{1,0:T(8,128)S(1)} %collective-permute-done.2.refs_0_, bf16[1024,256]{1,0:T(8,128)(2,1)S(1)} %get-tuple-element.28.refs_1_.refs_3_, f32[1,1024]{1,0:T(1,128)S(1)} %get-tuple-element.29.refs_2_.refs_4_, bf16[1024,256]{1,0:T(8,128)(2,1)S(1)} %get-tuple-element.30.refs_3_.refs_5_, ...), custom_call_target="tpu_custom_call" | custom-call | flops 1 | bytes 1 | tf_op jit(solution)/shard_map/pallas_call | solution.py:231
  15.8 0.0 collective-permute-done.4
  15.8 0.9 %shard_map.45 = f32[128,128]{1,0:T(8,128)S(1)} custom-call(f32[128,128]{1,0:T(8,128)S(1)} %broadcast_select_fusion.refs_0_, bf16[1024,256]{1,0:T(8,128)(2,1)S(1)} %get-tuple-element.28.refs_1_.refs_3_, f32[1,1024]{1,0:T(1,128)S(1)} %get-tuple-element.29.refs_2_.refs_4_, bf16[1024,256]{1,0:T(8,128)(2,1)S(1)} %get-tuple-element.30.refs_3_.refs_5_, ...), custom_call_target="tpu_custom_call" | custom-call | flops 1 | bytes 1 | tf_op jit(solution)/shard_map/pallas_call | solution.py:231
  16.7 0.0 collective-permute-done.5.refs_1_
  16.8 0.7 %collective-permute-start.6 = (f32[1024,128]{1,0:T(8,128)S(1)}, f32[1024,128]{1,0:T(8,128)S(1)}, u32[]{:S(2)}, u32[]{:S(2)}) collective-permute-start(f32[1024,128]{1,0:T(8,128)S(1)} %collective-permute-done.5.refs_1_), channel_id=1, source_target_pairs={{0,1},{1,0},{2,3},{3,2},{4,5},{5,4},{6,7},{7,6},{8,9},{9,8},{10,11... | collective-permute-start | bytes 1572872 | tf_op jit(solution)/shard_map/ppermute | solution.py:81
  17.5 0.1 collective-permute-start.7
  17.6 1.6 %shard_map.46 = (f32[512,128]{1,0:T(8,128)S(1)}, bf16[1024,256]{1,0:T(8,128)(2,1)S(1)}, f32[1,1024]{1,0:T(1,128)S(1)}) custom-call(f32[512,128]{1,0:T(8,128)S(1)} %pad_maximum_fusion.refs_0_.refs_1_, f32[1024,128]{1,0:T(8,128)S(1)} %collective-permute-done.5.refs_1_, f32[512,128]{1,0:T(8,128)S(1)} %pad_maximum_fusion.1.refs_2_), custom_call_target="tpu_custom_call" | custom-call | flops 1 | bytes 1 | tf_op jit(solution)/shard_map/pallas_call | solution.py:231
  19.1 0.2 collective-permute-done.7.refs_2_
  19.3 1.6 %shard_map.47 = (f32[512,128]{1,0:T(8,128)S(1)}, bf16[1024,256]{1,0:T(8,128)(2,1)}, f32[1,1024]{1,0:T(1,128)}) custom-call(f32[512,128]{1,0:T(8,128)S(1)} %pad_maximum_fusion.refs_0_.refs_1_, f32[512,128]{1,0:T(8,128)S(1)} %pad_maximum_fusion.refs_0_.refs_1_, f32[512,128]{1,0:T(8,128)S(1)} %collective-permute-done.7.refs_2_, ...), custom_call_target="tpu_custom_call" | custom-call | flops 1 | bytes 1 | tf_op jit(solution)/shard_map/pallas_call | solution.py:231
  21.0 0.0 collective-permute-done.6.refs_1_
  21.0 1.6 %shard_map.48 = (f32[512,128]{1,0:T(8,128)S(1)}, bf16[1024,256]{1,0:T(8,128)(2,1)S(1)}, f32[1,1024]{1,0:T(1,128)S(1)}) custom-call(f32[512,128]{1,0:T(8,128)S(1)} %pad_maximum_fusion.refs_0_.refs_1_, f32[1024,128]{1,0:T(8,128)S(1)} %collective-permute-done.6.refs_1_, f32[512,128]{1,0:T(8,128)S(1)} %get-tuple-element.39.refs_2_), custom_call_target="tpu_custom_call" | custom-call | flops 1 | bytes 1 | tf_op jit(solution)/shard_map/pallas_call | solution.py:231
  22.5 0.4 %collective-permute-start.8 = (f32[512,128]{1,0:T(8,128)S(1)}, f32[512,128]{1,0:T(8,128)S(1)}, u32[]{:S(2)}, u32[]{:S(2)}) collective-permute-start(f32[512,128]{1,0:T(8,128)S(1)} %get-tuple-element.40.refs_1_), channel_id=1, source_target_pairs={{0,1},{1,0},{2,3},{3,2},{4,5},{5,4},{6,7},{7,6},{8,9},{9,8},{10,11... | collective-permute-start | bytes 786440 | tf_op jit(solution)/shard_map/ppermute | solution.py:81
  23.0 1.2 %collective-permute-done.8.refs_2_ = f32[512,128]{1,0:T(8,128)S(1)} collective-permute-done((f32[512,128]{1,0:T(8,128)S(1)}, f32[512,128]{1,0:T(8,128)S(1)}, u32[]{:S(2)}, u32[]{:S(2)}) %collective-permute-start.8) | collective-permute-done | bytes 262176 | tf_op jit(solution)/shard_map/ppermute | solution.py:81
  24.1 2.4 %shard_map.49 = (f32[32,128]{1,0:T(8,128)}, f32[32,128]{1,0:T(8,128)}, bf16[1024,256]{1,0:T(8,128)(2,1)}, f32[1,1024]{1,0:T(1,128)}) custom-call(f32[32,128]{1,0:T(8,128)S(1)} %dynamic-slice_select_fusion.refs_0_, f32[512,128]{1,0:T(8,128)S(1)} %get-tuple-element.40.refs_1_, f32[512,128]{1,0:T(8,128)S(1)} %collective-permute-done.8.refs_2_, ...), custom_call_target="tpu_custom_call" | custom-call | flops 1 | bytes 1 | tf_op jit(solution)/shard_map/pallas_call | solution.py:231
  (6 shorter events, 0.1 us)
Async XLA Ops:
  0.6 8.3 %copy-start = (f32[1024,128]{1,0:T(8,128)S(1)}, f32[1024,128]{1,0:T(8,128)}, u32[]{:S(2)}) copy-start(f32[1024,128]{1,0:T(8,128)} %refs_1_.1) | copy-start | bytes 1572868
  0.6 7.6 %collective-permute-start.3 = (f32[1024,128]{1,0:T(8,128)}, f32[1024,128]{1,0:T(8,128)S(1)}, u32[]{:S(2)}, u32[]{:S(2)}) collective-permute-start(f32[1024,128]{1,0:T(8,128)} %refs_1_.1), channel_id=1, source_target_pairs={{0,1},{1,0},{2,3},{3,2},{4,5},{5,4},{6,7},{7,6},{8,9},{9,8},{10,11... | collective-permute-start | bytes 1572872 | tf_op jit(solution)/shard_map/ppermute | solution.py:81
  1.2 15.6 %collective-permute-start.5 = (f32[1024,128]{1,0:T(8,128)}, f32[1024,128]{1,0:T(8,128)S(1)}, u32[]{:S(2)}, u32[]{:S(2)}) collective-permute-start(f32[1024,128]{1,0:T(8,128)} %refs_1_.1), channel_id=1, source_target_pairs={{0,2},{1,3},{2,0},{3,1},{4,6},{5,7},{6,4},{7,5},{8,10},{9,11},{10,... | collective-permute-start | bytes 1572872 | tf_op jit(solution)/shard_map/ppermute | solution.py:81
  3.8 4.5 %collective-permute-start = (f32[128,128]{1,0:T(8,128)}, f32[128,128]{1,0:T(8,128)S(1)}, u32[]{:S(2)}, u32[]{:S(2)}) collective-permute-start(f32[128,128]{1,0:T(8,128)} %refs_5_.1), channel_id=1, source_target_pairs={{0,8},{1,5},{2,10},{3,7},{4,12},{5,1},{6,14},{7,3},{8,0},{9,13},{1... | collective-permute-start | bytes 196616 | tf_op jit(solution)/shard_map/ppermute | solution.py:247
  5.3 7.5 %collective-permute-start.1 = (f32[128,128]{1,0:T(8,128)}, f32[128,128]{1,0:T(8,128)S(1)}, u32[]{:S(2)}, u32[]{:S(2)}) collective-permute-start(f32[128,128]{1,0:T(8,128)} %refs_5_.1), channel_id=1, source_target_pairs={{0,24},{1,29},{2,26},{3,31},{4,28},{5,25},{6,30},{7,27},{8,16},{9,... | collective-permute-start | bytes 196616 | tf_op jit(solution)/shard_map/ppermute | solution.py:247
  7.8 7.0 %collective-permute-start.2 = (f32[128,128]{1,0:T(8,128)}, f32[128,128]{1,0:T(8,128)S(1)}, u32[]{:S(2)}, u32[]{:S(2)}) collective-permute-start(f32[128,128]{1,0:T(8,128)} %refs_5_.1), channel_id=1, source_target_pairs={{0,16},{1,21},{2,18},{3,23},{4,20},{5,17},{6,22},{7,19},{8,24},{9,... | collective-permute-start | bytes 196616 | tf_op jit(solution)/shard_map/ppermute | solution.py:247
  8.9 3.9 %copy-start.1 = (f32[128,128]{1,0:T(8,128)S(1)}, f32[128,128]{1,0:T(8,128)}, u32[]{:S(2)}) copy-start(f32[128,128]{1,0:T(8,128)} %refs_5_.1) | copy-start | bytes 196612
  9.6 6.2 %collective-permute-start.4 = (f32[128,128]{1,0:T(8,128)S(1)}, f32[128,128]{1,0:T(8,128)S(1)}, u32[]{:S(2)}, u32[]{:S(2)}) collective-permute-start(f32[128,128]{1,0:T(8,128)S(1)} %collective-permute-done.refs_0_), channel_id=1, source_target_pairs={{0,5},{2,7},{4,1},{6,3},{8,13},{10,15},{12,9},{14,11},{16,21},{18,... | collective-permute-start | bytes 196616 | tf_op jit(solution)/shard_map/ppermute | solution.py:272
  16.8 4.2 %collective-permute-start.6 = (f32[1024,128]{1,0:T(8,128)S(1)}, f32[1024,128]{1,0:T(8,128)S(1)}, u32[]{:S(2)}, u32[]{:S(2)}) collective-permute-start(f32[1024,128]{1,0:T(8,128)S(1)} %collective-permute-done.5.refs_1_), channel_id=1, source_target_pairs={{0,1},{1,0},{2,3},{3,2},{4,5},{5,4},{6,7},{7,6},{8,9},{9,8},{10,11... | collective-permute-start | bytes 1572872 | tf_op jit(solution)/shard_map/ppermute | solution.py:81
  17.5 1.9 %collective-permute-start.7 = (f32[512,128]{1,0:T(8,128)S(1)}, f32[512,128]{1,0:T(8,128)S(1)}, u32[]{:S(2)}, u32[]{:S(2)}) collective-permute-start(f32[512,128]{1,0:T(8,128)S(1)} %pad_maximum_fusion.refs_0_.refs_1_), channel_id=1, source_target_pairs={{0,1},{1,0},{2,3},{3,2},{4,5},{5,4},{6,7},{7,6},{8,9},{9,8},{10,11... | collective-permute-start | bytes 786440 | tf_op jit(solution)/shard_map/ppermute | solution.py:81
  22.5 1.6 %collective-permute-start.8 = (f32[512,128]{1,0:T(8,128)S(1)}, f32[512,128]{1,0:T(8,128)S(1)}, u32[]{:S(2)}, u32[]{:S(2)}) collective-permute-start(f32[512,128]{1,0:T(8,128)S(1)} %get-tuple-element.40.refs_1_), channel_id=1, source_target_pairs={{0,1},{1,0},{2,3},{3,2},{4,5},{5,4},{6,7},{7,6},{8,9},{9,8},{10,11... | collective-permute-start | bytes 786440 | tf_op jit(solution)/shard_map/ppermute | solution.py:81

commit v4 on v3

--- a/solution.py
+++ b/solution.py
@@ -170,7 +170,7 @@
     return (own_rows, (own_rows - start_rows) / step_size)
 
 
-def pull_kernel(scales, counts, has_first, moves, last, own_rows, *refs):
+def pull_kernel(scales, counts, has_first, moves, last, cut, prepares, *refs):
     refs = list(refs)
 
     def take(count):
@@ -180,16 +180,14 @@
     groups = [(take(raw), [tuple(take(2)) for _ in range(pairs)]) for raw, pairs in counts]
     first_refs = take(has_first)
     start_refs = take(last)
-    copied_refs = take(own_rows > 0)
+    whole_refs = take(cut)
+    prepare_refs = take(prepares)
     (out_ref,) = take(1)
+    drift_refs = take(last)
+    if cut:
+        cut_block(whole_refs[0], *take(3))
     rows = rows_ref[...]
     total = first_refs[0][...] if has_first else jnp.zeros(rows.shape, jnp.float32)
-    if last:
-        (drift_ref,) = take(1)
-    if copied_refs:
-        copy_ref, own_ref = take(2)
-        copy_ref[...] = copied_refs[0][...]
-        own_ref[...] = own_slice(copied_refs[0], own_rows)
     for scale, (raw, pairs) in zip(scales, groups):
         pieces = []
         if raw:
@@ -198,27 +196,48 @@
                 ref[...] = value
         pieces += [(right[...], square[...]) for right, square in pairs]
         total += all_terms(rows, pieces) * scale
+    if prepares:
+        for ref, value in zip(take(2), prepare(prepare_refs[0][...])):
+            ref[...] = value
     if moves:
         total = rows - step_size * total
     out_ref[...] = total
     if last:
-        drift_ref[...] = (total - start_refs[0][...]) / step_size
-
-
-def pull(rows, groups, first=None, moves=False, start=None, copied=None, own_rows=0):
+        drift_refs[0][...] = (total - start_refs[0][...]) / step_size
+
+
+def cut_block(block_ref, mine_ref, half_ref, start_ref):
+    place = lax.axis_index("ref")
+    core = lax.rem(place, 2)
+    rows, half = start_ref.shape[0], half_ref.shape[0]
+
+    def part(start, count):
+        return block_ref[pl.ds(pl.multiple_of(start, rows), count), :]
+
+    for i in range(mine_ref.shape[0] // rows):
+        mine_ref[pl.ds(i * rows, rows), :] = part((2 * i + core) * rows, rows)
+    half_ref[...] = part(core * half, half)
+    start_ref[...] = part(place * rows, rows)
+
+
+def pull(rows, groups, first=None, moves=False, start=None, cut=None, prepares=None):
     count, width = rows.shape
     args, outs = [rows], [f32(count, width)]
     if start is not None:
         outs.append(f32(count, width))
-    if copied is not None:
-        outs += [f32(*copied.shape), f32(own_rows, width)]
+    if cut is not None:
+        half = cut.shape[0] // 2
+        outs += [f32(half, width), f32(half, width), f32(cut.shape[0] // lax.axis_size("ref"), width)]
     results = len(outs)
     for _, raw, pairs in groups:
         args += list(raw) + [value for pair in pairs for value in pair]
         if raw:
             size = sum(r.shape[0] for r in raw)
             outs += [jax.ShapeDtypeStruct((size, 2 * width), jnp.bfloat16), f32(1, size)]
-    args += [value for value in (first, start, copied) if value is not None]
+    if prepares is not None:
+        size = prepares.shape[0]
+        outs += [jax.ShapeDtypeStruct((size, 2 * width), jnp.bfloat16), f32(1, size)]
+    args += [value for value in (first, start, cut, prepares) if value is not None]
     body = functools.partial(
         pull_kernel,
         [scale for scale, _, _ in groups],
@@ -226,7 +245,8 @@
         int(first is not None),
         moves,
         int(start is not None),
-        own_rows,
+        int(cut is not None),
+        int(prepares is not None),
     )
     got = pl.pallas_call(
         body,
@@ -255,45 +275,40 @@
     for_p = 1.0 / (block_rows * n_dom)
     for_r = -1.0 / (references.shape[0] * n_ref)
     place = lax.axis_index("ref")
-    core = place % 2
 
     across = exchange(references, "ref", 2)
-    near = by_core(particles, (2, 1), n_dom, n_ref)
+    near = by_core(particles, (2, 3), n_dom, n_ref)
     far = by_core(particles, (6, 7), n_dom, n_ref)
     middle = by_core(particles, (4, 5), n_dom, n_ref)
     mate = exchange(references, "ref", 1)
 
     near_sum, mate_pair = pull(near, [(for_r, [mate], [])])
-    near_sum, own_pair = pull(near, [(for_r, [references], [])], near_sum)
+    near_sum, mine, half, start_rows, own_pair = pull(
+        near, [(for_r, [references], [])], near_sum, cut=particles
+    )
     at_hand = [mate_pair, own_pair]
-    relay_pairs = [
-        (d * n_ref + r, (d ^ 1) * n_ref + r + 1) for d in range(n_dom) for r in range(0, n_ref, 2)
-    ]
-    relayed = lax.ppermute(after(near, near_sum), ("dom", "ref"), relay_pairs)
-    far_sum, block, start_rows = pull(
-        after(far, near_sum), [(for_r, [], at_hand)], copied=particles, own_rows=rows
-    )
-    middle_sum = pull(after(middle, far_sum), [(for_r, [], at_hand)])[0]
-    fourth = jnp.where(core == 0, block, after(relayed, middle_sum))
+    beside = exchange(half, "dom", 1)
+    far_sum = pull(after(far, near_sum), [(for_r, [], at_hand)])[0]
+    fourth = jnp.concatenate([mine, after(beside, far_sum)])
     fourth_sum = pull(fourth, [(for_r, [], at_hand)])[0]
-
-    held = jnp.concatenate([near, far, middle, fourth])
-    held_sum = jnp.concatenate([near_sum, far_sum, middle_sum, fourth_sum])
+    middle = after(middle, fourth_sum)
+    middle_sum = pull(middle, [(for_r, [], at_hand)])[0]
+
+    held = jnp.concatenate([near, far, fourth, middle])
+    held_sum = jnp.concatenate([near_sum, far_sum, fourth_sum, middle_sum])
     held_by_mate = exchange(held, "ref", 1)
-    across = after(across, fourth_sum)
+    across = after(across, middle_sum)
     across_mate = exchange(across, "ref", 1)
     held_sum, across_pair = pull(held, [(for_r, [across], [])], held_sum)
-    held_sum = pull(held, [(for_p, [held, held_by_mate], [])], held_sum)[0]
-    moved, across_mate_pair = pull(held, [(for_r, [across_mate], [])], held_sum, moves=True)
+    groups = [(for_p, [held, held_by_mate], []), (for_r, [across_mate], [])]
+    moved, _, across_mate_pair = pull(held, groups, held_sum, moves=True)
 
     moved_by_mate = exchange(moved, "ref", 1)
-    own_block = jnp.where(core == 0, moved[3 * block_rows :], moved_by_mate[3 * block_rows :])
-    own_rows = lax.dynamic_slice_in_dim(own_block, place * rows, rows, 0)
-    groups = [
-        (for_p, [moved, moved_by_mate], []),
-        (for_r, [], at_hand + [across_pair, across_mate_pair]),
-    ]
-    return tuple(pull(own_rows, groups, moves=True, start=start_rows)[:2])
+    own_rows = lax.dynamic_slice_in_dim(moved, 2 * block_rows + (place // 2) * rows, rows, 0)
+    groups = [(for_r, [], at_hand + [across_pair, across_mate_pair])]
+    own_sum, moved_pair = pull(own_rows, groups, prepares=moved)
+    groups = [(for_p, [moved_by_mate], [moved_pair])]
+    return tuple(pull(own_rows, groups, own_sum, moves=True, start=start_rows)[:2])
 
 
 def on_device(particles, references):

time: 26.7 us -> 24.5 us (0.918)
  starting transfers between devices: 11.7 us -> 9.01 us
  waiting for transfers between devices: 2.74 us -> 3.58 us
  Pallas kernels: 11.3 us -> 11 us
    ppermute x1 -> x0, starting transfers between devices: 3.21 us -> none  [gather_plan(): relayed = lax.ppermute(after(near, near_sum), ('dom', 'ref'), relay_pairs)]
    ppermute x3, waiting for transfers between devices: 1.34 us -> 2.23 us  [by_core(): return lax.ppermute(values, ('dom', 'ref'), pairs)]
    ppermute x5 -> x6, starting transfers between devices: 4.32 us -> 4.84 us  [exchange(): return lax.ppermute(values, axis, [(i, i ^ offset) for i in range(size)])]
    ppermute x5 -> x6, waiting for transfers between devices: 1.39 us -> 1.34 us  [exchange(): return lax.ppermute(values, axis, [(i, i ^ offset) for i in range(size)])]
  transfers between devices with their start and end apart: 9 -> 9, of which waited for: 4 -> 7; matrix products, arithmetic and copies ran while one was open for 0% -> 0% of each run, Pallas kernels for 28% -> 29%
where the time goes in v4:
time: 24.5 us; the launch traced here: 24.4 us
  Pallas kernels  11 us (45%)
  starting transfers between devices  9.01 us (37%)
  waiting for transfers between devices  3.58 us (15%)
  between operations  0.72 us (3%)
    pallas_call x9, Pallas kernels, pull(): pl.pallas_call(body, out_shape=outs, in_specs=[IN_VMEM] * len(args), out_...  11 us
    ppermute x6, starting transfers between devices, exchange(): return lax.ppermute(values, axis, [(i, i ^ offset) for i in range(size)])  4.84 us
    ppermute x3, starting transfers between devices, by_core(): return lax.ppermute(values, ('dom', 'ref'), pairs)  4.17 us
    ppermute x3, waiting for transfers between devices, by_core(): return lax.ppermute(values, ('dom', 'ref'), pairs)  2.23 us
    ppermute x6, waiting for transfers between devices, exchange(): return lax.ppermute(values, axis, [(i, i ^ offset) for i in range(size)])  1.34 us
  transfers between devices with their start and end apart: 9, of which 7 were waited for; matrix products, arithmetic and copies ran while one was open for 0% of the time, Pallas kernels for 29%

profile of v4, /device:TPU:0, one launch (start us, length us, event | category | flops | bytes accessed | tf_op | source)
XLA Modules:
  0.0 24.4 jit_solution(1826230023566701099)
XLA Ops:
  0.6 0.0 copy-start
  0.6 0.0 copy-start.1
  0.6 0.5 %collective-permute-start.2 = (f32[1024,128]{1,0:T(8,128)}, f32[1024,128]{1,0:T(8,128)S(1)}, u32[]{:S(2)}, u32[]{:S(2)}) collective-permute-start(f32[1024,128]{1,0:T(8,128)} %refs_1_.1), channel_id=1, source_target_pairs={{0,1},{1,0},{2,3},{3,2},{4,5},{5,4},{6,7},{7,6},{8,9},{9,8},{10,11... | collective-permute-start | bytes 1572872 | tf_op jit(solution)/shard_map/ppermute | solution.py:81
  1.2 2.6 %collective-permute-start.6 = (f32[1024,128]{1,0:T(8,128)}, f32[1024,128]{1,0:T(8,128)S(1)}, u32[]{:S(2)}, u32[]{:S(2)}) collective-permute-start(f32[1024,128]{1,0:T(8,128)} %refs_1_.1), channel_id=1, source_target_pairs={{0,2},{1,3},{2,0},{3,1},{4,6},{5,7},{6,4},{7,5},{8,10},{9,11},{10,... | collective-permute-start | bytes 1572872 | tf_op jit(solution)/shard_map/ppermute | solution.py:81
  3.8 1.6 %collective-permute-start = (f32[128,128]{1,0:T(8,128)}, f32[128,128]{1,0:T(8,128)S(1)}, u32[]{:S(2)}, u32[]{:S(2)}) collective-permute-start(f32[128,128]{1,0:T(8,128)} %refs_3_.1), channel_id=1, source_target_pairs={{0,8},{1,13},{2,10},{3,15},{4,12},{5,9},{6,14},{7,11},{8,0},{9,5},... | collective-permute-start | bytes 196616 | tf_op jit(solution)/shard_map/ppermute | solution.py:267
  5.3 2.5 %collective-permute-start.1 = (f32[128,128]{1,0:T(8,128)}, f32[128,128]{1,0:T(8,128)S(1)}, u32[]{:S(2)}, u32[]{:S(2)}) collective-permute-start(f32[128,128]{1,0:T(8,128)} %refs_3_.1), channel_id=1, source_target_pairs={{0,24},{1,29},{2,26},{3,31},{4,28},{5,25},{6,30},{7,27},{8,16},{9,... | collective-permute-start | bytes 196616 | tf_op jit(solution)/shard_map/ppermute | solution.py:267
  7.8 0.1 collective-permute-start.4
  7.9 0.9 %collective-permute-done.refs_0_ = f32[128,128]{1,0:T(8,128)S(1)} collective-permute-done((f32[128,128]{1,0:T(8,128)}, f32[128,128]{1,0:T(8,128)S(1)}, u32[]{:S(2)}, u32[]{:S(2)}) %collective-permute-start) | collective-permute-done | bytes 65568 | tf_op jit(solution)/shard_map/ppermute | solution.py:267
  8.8 0.0 collective-permute-done.2.refs_1_
  8.8 0.7 %shard_map.41 = (f32[128,128]{1,0:T(8,128)S(1)}, bf16[1024,256]{1,0:T(8,128)(2,1)S(1)}, f32[1,1024]{1,0:T(1,128)S(1)}) custom-call(f32[128,128]{1,0:T(8,128)S(1)} %collective-permute-done.refs_0_, f32[1024,128]{1,0:T(8,128)S(1)} %collective-permute-done.2.refs_1_), custom_call_target="tpu_custom_call" | custom-call | flops 1 | bytes 1 | tf_op jit(solution)/shard_map/pallas_call | solution.py:251
  9.5 0.0 copy-done
  9.5 0.0 copy-done.1
  9.5 0.7 %shard_map.42 = (f32[128,128]{1,0:T(8,128)S(1)}, f32[64,128]{1,0:T(8,128)S(1)}, f32[64,128]{1,0:T(8,128)S(1)}, f32[32,128]{1,0:T(8,128)S(1)}, bf16[1024,256]{1,0:T(8,128)(2,1)S(1)}, /*index=5*/f32[1,1024]{1,0:T(1,128)S(1)}) custom-call(f32[128,128]{1,0:T(8,128)S(1)} %collective-permute-done.refs_0_, f32[1024,128]{1,0:T(8,128)S(1)} %copy-done, ...), custom_call_target="tpu_custom_call" | custom-call | flops 1 | bytes 1 | tf_op jit(solution)/shard_map/pallas_call | solution.py:251
  10.2 1.0 %collective-permute-start.3 = (f32[64,128]{1,0:T(8,128)S(1)}, f32[64,128]{1,0:T(8,128)S(1)}, u32[]{:S(2)}, u32[]{:S(2)}) collective-permute-start(f32[64,128]{1,0:T(8,128)S(1)} %get-tuple-element.28), channel_id=1, source_target_pairs={{0,4},{4,0},{8,12},{12,8},{16,20},{20,16},{24,28},{28,24},{1,5},{5... | collective-permute-start | bytes 98312 | tf_op jit(solution)/shard_map/ppermute | solution.py:81
  11.2 1.2 %collective-permute-done.1.refs_0_ = f32[128,128]{1,0:T(8,128)S(1)} collective-permute-done((f32[128,128]{1,0:T(8,128)}, f32[128,128]{1,0:T(8,128)S(1)}, u32[]{:S(2)}, u32[]{:S(2)}) %collective-permute-start.1) | collective-permute-done | bytes 65568 | tf_op jit(solution)/shard_map/ppermute | solution.py:267
  12.4 0.9 %shard_map.43 = f32[128,128]{1,0:T(8,128)S(1)} custom-call(f32[128,128]{1,0:T(8,128)S(1)} %collective-permute-done.1.refs_0_, bf16[1024,256]{1,0:T(8,128)(2,1)S(1)} %get-tuple-element.31.refs_1_, f32[1,1024]{1,0:T(1,128)S(1)} %get-tuple-element.32.refs_2_, bf16[1024,256]{1,0:T(8,128)(2,1)S(1)} %get-tuple-element.33.refs_3_, ...), custom_call_target="tpu_custom_call" | custom-call | flops 1 | bytes 1 | tf_op jit(solution)/shard_map/pallas_call | solution.py:251
  13.4 0.8 %collective-permute-done.3 = f32[64,128]{1,0:T(8,128)S(1)} collective-permute-done((f32[64,128]{1,0:T(8,128)S(1)}, f32[64,128]{1,0:T(8,128)S(1)}, u32[]{:S(2)}, u32[]{:S(2)}) %collective-permute-start.3) | collective-permute-done | bytes 32800 | tf_op jit(solution)/shard_map/ppermute | solution.py:81
  14.2 0.9 %shard_map.44 = f32[128,128]{1,0:T(8,128)S(1)} custom-call(f32[128,128]{1,0:T(8,128)S(1)} %pad_maximum_fusion.1.refs_0_, bf16[1024,256]{1,0:T(8,128)(2,1)S(1)} %get-tuple-element.31.refs_1_, f32[1,1024]{1,0:T(1,128)S(1)} %get-tuple-element.32.refs_2_, bf16[1024,256]{1,0:T(8,128)(2,1)S(1)} %get-tuple-element.33.refs_3_, f32[1,1024]{1,0:T(1,128)S(1)} %get-tuple-element.34.refs_4_), custom_call_target="tpu_custom_call" | custom-call | flops 1 | bytes 1 | tf_op jit(solution)/shard_map/pallas_call | solution.py:251
  15.1 0.1 collective-permute-done.4.refs_0_
  15.2 0.9 %shard_map.45 = f32[128,128]{1,0:T(8,128)S(1)} custom-call(f32[128,128]{1,0:T(8,128)S(1)} %collective-permute-done.4.refs_0_, bf16[1024,256]{1,0:T(8,128)(2,1)S(1)} %get-tuple-element.31.refs_1_, f32[1,1024]{1,0:T(1,128)S(1)} %get-tuple-element.32.refs_2_, bf16[1024,256]{1,0:T(8,128)(2,1)S(1)} %get-tuple-element.33.refs_3_, ...), custom_call_target="tpu_custom_call" | custom-call | flops 1 | bytes 1 | tf_op jit(solution)/shard_map/pallas_call | solution.py:251
  16.2 0.3 %collective-permute-done.6.refs_1_ = f32[1024,128]{1,0:T(8,128)S(1)} collective-permute-done((f32[1024,128]{1,0:T(8,128)}, f32[1024,128]{1,0:T(8,128)S(1)}, u32[]{:S(2)}, u32[]{:S(2)}) %collective-permute-start.6) | collective-permute-done | bytes 524320 | tf_op jit(solution)/shard_map/ppermute | solution.py:81
  16.5 0.2 collective-permute-start.7
  16.7 0.4 %collective-permute-start.5 = (f32[512,128]{1,0:T(8,128)S(1)}, f32[512,128]{1,0:T(8,128)S(1)}, u32[]{:S(2)}, u32[]{:S(2)}) collective-permute-start(f32[512,128]{1,0:T(8,128)S(1)} %constant_dynamic-update-slice_fusion.refs_0_.refs_1_), channel_id=1, source_target_pairs={{0,1},{1,0},{2,3},{3,2},{4,5},{5,4},{6,7},{7,6},{8,9},{9,8},{10,11... | collective-permute-start | bytes 786440 | tf_op jit(solution)/shard_map/ppermute | solution.py:81
  17.1 1.6 %shard_map.46 = (f32[512,128]{1,0:T(8,128)S(1)}, bf16[1024,256]{1,0:T(8,128)(2,1)S(1)}, f32[1,1024]{1,0:T(1,128)S(1)}) custom-call(f32[512,128]{1,0:T(8,128)S(1)} %constant_dynamic-update-slice_fusion.refs_0_.refs_1_, f32[1024,128]{1,0:T(8,128)S(1)} %collective-permute-done.6.refs_1_, f32[512,128]{1,0:T(8,128)S(1)} %pad_maximum_fusion.refs_2_), custom_call_target="tpu_custom_call" | custom-call | flops 1 | bytes 1 | tf_op jit(solution)/shard_map/pallas_call | solution.py:251
  18.7 0.1 collective-permute-done.5.refs_2_
  18.8 0.0 collective-permute-done.7.refs_3_
  18.8 2.7 %shard_map.47 = (f32[512,128]{1,0:T(8,128)S(1)}, bf16[1024,256]{1,0:T(8,128)(2,1)}, f32[1,1024]{1,0:T(1,128)}, bf16[1024,256]{1,0:T(8,128)(2,1)S(1)}, f32[1,1024]{1,0:T(1,128)S(1)}) custom-call(f32[512,128]{1,0:T(8,128)S(1)} %constant_dynamic-update-slice_fusion.refs_0_.refs_1_, f32[512,128]{1,0:T(8,128)S(1)} %constant_dynamic-update-slice_fusion.refs_0_.refs_1_, ...), custom_call_target="tpu_custom_call" | custom-call | flops 1 | bytes 1 | tf_op jit(solution)/shard_map/pallas_call | solution.py:251
  21.5 0.2 collective-permute-start.8
  21.7 1.3 %shard_map.48 = (f32[32,128]{1,0:T(8,128)S(1)}, bf16[512,256]{1,0:T(8,128)(2,1)S(1)}, f32[1,512]{1,0:T(1,128)S(1)}) custom-call(f32[32,128]{1,0:T(8,128)S(1)} %constant_dynamic-slice_fusion.refs_0_, bf16[1024,256]{1,0:T(8,128)(2,1)S(1)} %get-tuple-element.31.refs_1_, f32[1,1024]{1,0:T(1,128)S(1)} %get-tuple-element.32.refs_2_, ...), custom_call_target="tpu_custom_call" | custom-call | flops 1 | bytes 1 | tf_op jit(solution)/shard_map/pallas_call | solution.py:251
  22.9 0.1 collective-permute-done.8.refs_1_
  23.1 1.3 %shard_map.49 = (f32[32,128]{1,0:T(8,128)}, f32[32,128]{1,0:T(8,128)}, bf16[512,256]{1,0:T(8,128)(2,1)}, f32[1,512]{1,0:T(1,128)}) custom-call(f32[32,128]{1,0:T(8,128)S(1)} %constant_dynamic-slice_fusion.refs_0_, f32[512,128]{1,0:T(8,128)S(1)} %collective-permute-done.8.refs_1_, bf16[512,256]{1,0:T(8,128)(2,1)S(1)} %get-tuple-element.44.refs_2_, ...), custom_call_target="tpu_custom_call" | custom-call | flops 1 | bytes 1 | tf_op jit(solution)/shard_map/pallas_call | solution.py:251
  (8 shorter events, 0.1 us)
Async XLA Ops:
  0.6 8.9 %copy-start = (f32[1024,128]{1,0:T(8,128)S(1)}, f32[1024,128]{1,0:T(8,128)}, u32[]{:S(2)}) copy-start(f32[1024,128]{1,0:T(8,128)} %refs_1_.1) | copy-start | bytes 1572868
  0.6 8.9 %copy-start.1 = (f32[128,128]{1,0:T(8,128)S(1)}, f32[128,128]{1,0:T(8,128)}, u32[]{:S(2)}) copy-start(f32[128,128]{1,0:T(8,128)} %refs_3_.1) | copy-start | bytes 196612
  0.6 8.2 %collective-permute-start.2 = (f32[1024,128]{1,0:T(8,128)}, f32[1024,128]{1,0:T(8,128)S(1)}, u32[]{:S(2)}, u32[]{:S(2)}) collective-permute-start(f32[1024,128]{1,0:T(8,128)} %refs_1_.1), channel_id=1, source_target_pairs={{0,1},{1,0},{2,3},{3,2},{4,5},{5,4},{6,7},{7,6},{8,9},{9,8},{10,11... | collective-permute-start | bytes 1572872 | tf_op jit(solution)/shard_map/ppermute | solution.py:81
  1.2 15.3 %collective-permute-start.6 = (f32[1024,128]{1,0:T(8,128)}, f32[1024,128]{1,0:T(8,128)S(1)}, u32[]{:S(2)}, u32[]{:S(2)}) collective-permute-start(f32[1024,128]{1,0:T(8,128)} %refs_1_.1), channel_id=1, source_target_pairs={{0,2},{1,3},{2,0},{3,1},{4,6},{5,7},{6,4},{7,5},{8,10},{9,11},{10,... | collective-permute-start | bytes 1572872 | tf_op jit(solution)/shard_map/ppermute | solution.py:81
  3.8 5.1 %collective-permute-start = (f32[128,128]{1,0:T(8,128)}, f32[128,128]{1,0:T(8,128)S(1)}, u32[]{:S(2)}, u32[]{:S(2)}) collective-permute-start(f32[128,128]{1,0:T(8,128)} %refs_3_.1), channel_id=1, source_target_pairs={{0,8},{1,13},{2,10},{3,15},{4,12},{5,9},{6,14},{7,11},{8,0},{9,5},... | collective-permute-start | bytes 196616 | tf_op jit(solution)/shard_map/ppermute | solution.py:267
  5.3 7.1 %collective-permute-start.1 = (f32[128,128]{1,0:T(8,128)}, f32[128,128]{1,0:T(8,128)S(1)}, u32[]{:S(2)}, u32[]{:S(2)}) collective-permute-start(f32[128,128]{1,0:T(8,128)} %refs_3_.1), channel_id=1, source_target_pairs={{0,24},{1,29},{2,26},{3,31},{4,28},{5,25},{6,30},{7,27},{8,16},{9,... | collective-permute-start | bytes 196616 | tf_op jit(solution)/shard_map/ppermute | solution.py:267
  7.8 7.4 %collective-permute-start.4 = (f32[128,128]{1,0:T(8,128)}, f32[128,128]{1,0:T(8,128)S(1)}, u32[]{:S(2)}, u32[]{:S(2)}) collective-permute-start(f32[128,128]{1,0:T(8,128)} %refs_3_.1), channel_id=1, source_target_pairs={{0,16},{1,21},{2,18},{3,23},{4,20},{5,17},{6,22},{7,19},{8,24},{9,... | collective-permute-start | bytes 196616 | tf_op jit(solution)/shard_map/ppermute | solution.py:267
  10.2 4.0 %collective-permute-start.3 = (f32[64,128]{1,0:T(8,128)S(1)}, f32[64,128]{1,0:T(8,128)S(1)}, u32[]{:S(2)}, u32[]{:S(2)}) collective-permute-start(f32[64,128]{1,0:T(8,128)S(1)} %get-tuple-element.28), channel_id=1, source_target_pairs={{0,4},{4,0},{8,12},{12,8},{16,20},{20,16},{24,28},{28,24},{1,5},{5... | collective-permute-start | bytes 98312 | tf_op jit(solution)/shard_map/ppermute | solution.py:81
  16.5 2.3 %collective-permute-start.7 = (f32[1024,128]{1,0:T(8,128)S(1)}, f32[1024,128]{1,0:T(8,128)S(1)}, u32[]{:S(2)}, u32[]{:S(2)}) collective-permute-start(f32[1024,128]{1,0:T(8,128)S(1)} %collective-permute-done.6.refs_1_), channel_id=1, source_target_pairs={{0,1},{1,0},{2,3},{3,2},{4,5},{5,4},{6,7},{7,6},{8,9},{9,8},{10,11... | collective-permute-start | bytes 1572872 | tf_op jit(solution)/shard_map/ppermute | solution.py:81
  16.7 2.1 %collective-permute-start.5 = (f32[512,128]{1,0:T(8,128)S(1)}, f32[512,128]{1,0:T(8,128)S(1)}, u32[]{:S(2)}, u32[]{:S(2)}) collective-permute-start(f32[512,128]{1,0:T(8,128)S(1)} %constant_dynamic-update-slice_fusion.refs_0_.refs_1_), channel_id=1, source_target_pairs={{0,1},{1,0},{2,3},{3,2},{4,5},{5,4},{6,7},{7,6},{8,9},{9,8},{10,11... | collective-permute-start | bytes 786440 | tf_op jit(solution)/shard_map/ppermute | solution.py:81
  21.5 1.5 %collective-permute-start.8 = (f32[512,128]{1,0:T(8,128)S(1)}, f32[512,128]{1,0:T(8,128)S(1)}, u32[]{:S(2)}, u32[]{:S(2)}) collective-permute-start(f32[512,128]{1,0:T(8,128)S(1)} %get-tuple-element.39.refs_9_), channel_id=1, source_target_pairs={{0,1},{1,0},{2,3},{3,2},{4,5},{5,4},{6,7},{7,6},{8,9},{9,8},{10,11... | collective-permute-start | bytes 786440 | tf_op jit(solution)/shard_map/ppermute | solution.py:81

commit v5 on v4

--- a/solution.py
+++ b/solution.py
@@ -276,7 +276,7 @@
     for_r = -1.0 / (references.shape[0] * n_ref)
     place = lax.axis_index("ref")
 
-    across = exchange(references, "ref", 2)
+    across = exchange(references, "ref", 3)
     near = by_core(particles, (2, 3), n_dom, n_ref)
     far = by_core(particles, (6, 7), n_dom, n_ref)
     middle = by_core(particles, (4, 5), n_dom, n_ref)

time: 24.5 us -> 24.4 us (level)
  waiting for transfers between devices: 3.58 us -> 3.28 us
    ppermute x6, waiting for transfers between devices: 1.34 us -> 1.04 us  [exchange(): return lax.ppermute(values, axis, [(i, i ^ offset) for i in range(size)])]
  transfers between devices with their start and end apart: 9 -> 9, of which waited for: 7 -> 4; matrix products, arithmetic and copies ran while one was open for 0% -> 0% of each run, Pallas kernels for 29% -> 29%
where the time goes in v5:
time: 24.4 us; the launch traced here: 24.3 us
  Pallas kernels  11 us (45%)
  starting transfers between devices  9.13 us (37%)
  waiting for transfers between devices  3.28 us (13%)
  between operations  0.74 us (3%)
    pallas_call x9, Pallas kernels, pull(): pl.pallas_call(body, out_shape=outs, in_specs=[IN_VMEM] * len(args), out_...  11 us
    ppermute x6, starting transfers between devices, exchange(): return lax.ppermute(values, axis, [(i, i ^ offset) for i in range(size)])  4.96 us
    ppermute x3, starting transfers between devices, by_core(): return lax.ppermute(values, ('dom', 'ref'), pairs)  4.17 us
    ppermute x3, waiting for transfers between devices, by_core(): return lax.ppermute(values, ('dom', 'ref'), pairs)  2.25 us
    ppermute x6, waiting for transfers between devices, exchange(): return lax.ppermute(values, axis, [(i, i ^ offset) for i in range(size)])  1.04 us
  transfers between devices with their start and end apart: 9, of which 4 were waited for; matrix products, arithmetic and copies ran while one was open for 0% of the time, Pallas kernels for 29%

profile of v5, /device:TPU:0, one launch (start us, length us, event | category | flops | bytes accessed | tf_op | source)
XLA Modules:
  0.0 24.3 jit_solution(1949553253204968693)
XLA Ops:
  0.6 0.0 copy-start
  0.6 0.0 copy-start.1
  0.6 0.5 %collective-permute-start.2 = (f32[1024,128]{1,0:T(8,128)}, f32[1024,128]{1,0:T(8,128)S(1)}, u32[]{:S(2)}, u32[]{:S(2)}) collective-permute-start(f32[1024,128]{1,0:T(8,128)} %refs_1_.1), channel_id=1, source_target_pairs={{0,1},{1,0},{2,3},{3,2},{4,5},{5,4},{6,7},{7,6},{8,9},{9,8},{10,11... | collective-permute-start | bytes 1572872 | tf_op jit(solution)/shard_map/ppermute | solution.py:81
  1.2 2.6 %collective-permute-start.6 = (f32[1024,128]{1,0:T(8,128)}, f32[1024,128]{1,0:T(8,128)S(1)}, u32[]{:S(2)}, u32[]{:S(2)}) collective-permute-start(f32[1024,128]{1,0:T(8,128)} %refs_1_.1), channel_id=1, source_target_pairs={{0,3},{1,2},{2,1},{3,0},{4,7},{5,6},{6,5},{7,4},{8,11},{9,10},{10,... | collective-permute-start | bytes 1572872 | tf_op jit(solution)/shard_map/ppermute | solution.py:81
  3.8 1.6 %collective-permute-start = (f32[128,128]{1,0:T(8,128)}, f32[128,128]{1,0:T(8,128)S(1)}, u32[]{:S(2)}, u32[]{:S(2)}) collective-permute-start(f32[128,128]{1,0:T(8,128)} %refs_3_.1), channel_id=1, source_target_pairs={{0,8},{1,13},{2,10},{3,15},{4,12},{5,9},{6,14},{7,11},{8,0},{9,5},... | collective-permute-start | bytes 196616 | tf_op jit(solution)/shard_map/ppermute | solution.py:267
  5.4 2.5 %collective-permute-start.1 = (f32[128,128]{1,0:T(8,128)}, f32[128,128]{1,0:T(8,128)S(1)}, u32[]{:S(2)}, u32[]{:S(2)}) collective-permute-start(f32[128,128]{1,0:T(8,128)} %refs_3_.1), channel_id=1, source_target_pairs={{0,24},{1,29},{2,26},{3,31},{4,28},{5,25},{6,30},{7,27},{8,16},{9,... | collective-permute-start | bytes 196616 | tf_op jit(solution)/shard_map/ppermute | solution.py:267
  7.9 0.1 collective-permute-start.4
  8.0 1.0 %collective-permute-done.refs_0_ = f32[128,128]{1,0:T(8,128)S(1)} collective-permute-done((f32[128,128]{1,0:T(8,128)}, f32[128,128]{1,0:T(8,128)S(1)}, u32[]{:S(2)}, u32[]{:S(2)}) %collective-permute-start) | collective-permute-done | bytes 65568 | tf_op jit(solution)/shard_map/ppermute | solution.py:267
  9.0 0.0 collective-permute-done.2.refs_1_
  9.0 0.7 %shard_map.41 = (f32[128,128]{1,0:T(8,128)S(1)}, bf16[1024,256]{1,0:T(8,128)(2,1)S(1)}, f32[1,1024]{1,0:T(1,128)S(1)}) custom-call(f32[128,128]{1,0:T(8,128)S(1)} %collective-permute-done.refs_0_, f32[1024,128]{1,0:T(8,128)S(1)} %collective-permute-done.2.refs_1_), custom_call_target="tpu_custom_call" | custom-call | flops 1 | bytes 1 | tf_op jit(solution)/shard_map/pallas_call | solution.py:251
  9.7 0.0 copy-done
  9.7 0.0 copy-done.1
  9.7 0.7 %shard_map.42 = (f32[128,128]{1,0:T(8,128)S(1)}, f32[64,128]{1,0:T(8,128)S(1)}, f32[64,128]{1,0:T(8,128)S(1)}, f32[32,128]{1,0:T(8,128)S(1)}, bf16[1024,256]{1,0:T(8,128)(2,1)S(1)}, /*index=5*/f32[1,1024]{1,0:T(1,128)S(1)}) custom-call(f32[128,128]{1,0:T(8,128)S(1)} %collective-permute-done.refs_0_, f32[1024,128]{1,0:T(8,128)S(1)} %copy-done, ...), custom_call_target="tpu_custom_call" | custom-call | flops 1 | bytes 1 | tf_op jit(solution)/shard_map/pallas_call | solution.py:251
  10.4 0.9 %collective-permute-start.3 = (f32[64,128]{1,0:T(8,128)S(1)}, f32[64,128]{1,0:T(8,128)S(1)}, u32[]{:S(2)}, u32[]{:S(2)}) collective-permute-start(f32[64,128]{1,0:T(8,128)S(1)} %get-tuple-element.28), channel_id=1, source_target_pairs={{0,4},{4,0},{8,12},{12,8},{16,20},{20,16},{24,28},{28,24},{1,5},{5... | collective-permute-start | bytes 98312 | tf_op jit(solution)/shard_map/ppermute | solution.py:81
  11.2 1.3 %collective-permute-done.1.refs_0_ = f32[128,128]{1,0:T(8,128)S(1)} collective-permute-done((f32[128,128]{1,0:T(8,128)}, f32[128,128]{1,0:T(8,128)S(1)}, u32[]{:S(2)}, u32[]{:S(2)}) %collective-permute-start.1) | collective-permute-done | bytes 65568 | tf_op jit(solution)/shard_map/ppermute | solution.py:267
  12.5 0.9 %shard_map.43 = f32[128,128]{1,0:T(8,128)S(1)} custom-call(f32[128,128]{1,0:T(8,128)S(1)} %collective-permute-done.1.refs_0_, bf16[1024,256]{1,0:T(8,128)(2,1)S(1)} %get-tuple-element.31.refs_1_, f32[1,1024]{1,0:T(1,128)S(1)} %get-tuple-element.32.refs_2_, bf16[1024,256]{1,0:T(8,128)(2,1)S(1)} %get-tuple-element.33.refs_3_, ...), custom_call_target="tpu_custom_call" | custom-call | flops 1 | bytes 1 | tf_op jit(solution)/shard_map/pallas_call | solution.py:251
  13.4 0.9 %collective-permute-done.3 = f32[64,128]{1,0:T(8,128)S(1)} collective-permute-done((f32[64,128]{1,0:T(8,128)S(1)}, f32[64,128]{1,0:T(8,128)S(1)}, u32[]{:S(2)}, u32[]{:S(2)}) %collective-permute-start.3) | collective-permute-done | bytes 32800 | tf_op jit(solution)/shard_map/ppermute | solution.py:81
  14.4 0.9 %shard_map.44 = f32[128,128]{1,0:T(8,128)S(1)} custom-call(f32[128,128]{1,0:T(8,128)S(1)} %pad_maximum_fusion.1.refs_0_, bf16[1024,256]{1,0:T(8,128)(2,1)S(1)} %get-tuple-element.31.refs_1_, f32[1,1024]{1,0:T(1,128)S(1)} %get-tuple-element.32.refs_2_, bf16[1024,256]{1,0:T(8,128)(2,1)S(1)} %get-tuple-element.33.refs_3_, f32[1,1024]{1,0:T(1,128)S(1)} %get-tuple-element.34.refs_4_), custom_call_target="tpu_custom_call" | custom-call | flops 1 | bytes 1 | tf_op jit(solution)/shard_map/pallas_call | solution.py:251
  15.3 0.0 collective-permute-done.4.refs_0_
  15.3 0.9 %shard_map.45 = f32[128,128]{1,0:T(8,128)S(1)} custom-call(f32[128,128]{1,0:T(8,128)S(1)} %collective-permute-done.4.refs_0_, bf16[1024,256]{1,0:T(8,128)(2,1)S(1)} %get-tuple-element.31.refs_1_, f32[1,1024]{1,0:T(1,128)S(1)} %get-tuple-element.32.refs_2_, bf16[1024,256]{1,0:T(8,128)(2,1)S(1)} %get-tuple-element.33.refs_3_, ...), custom_call_target="tpu_custom_call" | custom-call | flops 1 | bytes 1 | tf_op jit(solution)/shard_map/pallas_call | solution.py:251
  16.2 0.0 collective-permute-done.6.refs_1_
  16.2 0.3 %collective-permute-start.7 = (f32[1024,128]{1,0:T(8,128)S(1)}, f32[1024,128]{1,0:T(8,128)S(1)}, u32[]{:S(2)}, u32[]{:S(2)}) collective-permute-start(f32[1024,128]{1,0:T(8,128)S(1)} %collective-permute-done.6.refs_1_), channel_id=1, source_target_pairs={{0,1},{1,0},{2,3},{3,2},{4,5},{5,4},{6,7},{7,6},{8,9},{9,8},{10,11... | collective-permute-start | bytes 1572872 | tf_op jit(solution)/shard_map/ppermute | solution.py:81
  16.6 0.3 %collective-permute-start.5 = (f32[512,128]{1,0:T(8,128)S(1)}, f32[512,128]{1,0:T(8,128)S(1)}, u32[]{:S(2)}, u32[]{:S(2)}) collective-permute-start(f32[512,128]{1,0:T(8,128)S(1)} %constant_dynamic-update-slice_fusion.refs_0_.refs_1_), channel_id=1, source_target_pairs={{0,1},{1,0},{2,3},{3,2},{4,5},{5,4},{6,7},{7,6},{8,9},{9,8},{10,11... | collective-permute-start | bytes 786440 | tf_op jit(solution)/shard_map/ppermute | solution.py:81
  16.9 1.6 %shard_map.46 = (f32[512,128]{1,0:T(8,128)S(1)}, bf16[1024,256]{1,0:T(8,128)(2,1)S(1)}, f32[1,1024]{1,0:T(1,128)S(1)}) custom-call(f32[512,128]{1,0:T(8,128)S(1)} %constant_dynamic-update-slice_fusion.refs_0_.refs_1_, f32[1024,128]{1,0:T(8,128)S(1)} %collective-permute-done.6.refs_1_, f32[512,128]{1,0:T(8,128)S(1)} %pad_maximum_fusion.refs_2_), custom_call_target="tpu_custom_call" | custom-call | flops 1 | bytes 1 | tf_op jit(solution)/shard_map/pallas_call | solution.py:251
  18.5 0.1 collective-permute-done.5.refs_2_
  18.6 0.0 collective-permute-done.7.refs_3_
  18.6 2.7 %shard_map.47 = (f32[512,128]{1,0:T(8,128)S(1)}, bf16[1024,256]{1,0:T(8,128)(2,1)}, f32[1,1024]{1,0:T(1,128)}, bf16[1024,256]{1,0:T(8,128)(2,1)S(1)}, f32[1,1024]{1,0:T(1,128)S(1)}) custom-call(f32[512,128]{1,0:T(8,128)S(1)} %constant_dynamic-update-slice_fusion.refs_0_.refs_1_, f32[512,128]{1,0:T(8,128)S(1)} %constant_dynamic-update-slice_fusion.refs_0_.refs_1_, ...), custom_call_target="tpu_custom_call" | custom-call | flops 1 | bytes 1 | tf_op jit(solution)/shard_map/pallas_call | solution.py:251
  21.3 0.3 %collective-permute-start.8 = (f32[512,128]{1,0:T(8,128)S(1)}, f32[512,128]{1,0:T(8,128)S(1)}, u32[]{:S(2)}, u32[]{:S(2)}) collective-permute-start(f32[512,128]{1,0:T(8,128)S(1)} %get-tuple-element.39.refs_9_), channel_id=1, source_target_pairs={{0,1},{1,0},{2,3},{3,2},{4,5},{5,4},{6,7},{7,6},{8,9},{9,8},{10,11... | collective-permute-start | bytes 786440 | tf_op jit(solution)/shard_map/ppermute | solution.py:81
  21.6 1.3 %shard_map.48 = (f32[32,128]{1,0:T(8,128)S(1)}, bf16[512,256]{1,0:T(8,128)(2,1)S(1)}, f32[1,512]{1,0:T(1,128)S(1)}) custom-call(f32[32,128]{1,0:T(8,128)S(1)} %constant_dynamic-slice_fusion.refs_0_, bf16[1024,256]{1,0:T(8,128)(2,1)S(1)} %get-tuple-element.31.refs_1_, f32[1,1024]{1,0:T(1,128)S(1)} %get-tuple-element.32.refs_2_, ...), custom_call_target="tpu_custom_call" | custom-call | flops 1 | bytes 1 | tf_op jit(solution)/shard_map/pallas_call | solution.py:251
  22.9 0.0 collective-permute-done.8.refs_1_
  22.9 1.3 %shard_map.49 = (f32[32,128]{1,0:T(8,128)}, f32[32,128]{1,0:T(8,128)}, bf16[512,256]{1,0:T(8,128)(2,1)}, f32[1,512]{1,0:T(1,128)}) custom-call(f32[32,128]{1,0:T(8,128)S(1)} %constant_dynamic-slice_fusion.refs_0_, f32[512,128]{1,0:T(8,128)S(1)} %collective-permute-done.8.refs_1_, bf16[512,256]{1,0:T(8,128)(2,1)S(1)} %get-tuple-element.44.refs_2_, ...), custom_call_target="tpu_custom_call" | custom-call | flops 1 | bytes 1 | tf_op jit(solution)/shard_map/pallas_call | solution.py:251
  (8 shorter events, 0.1 us)
Async XLA Ops:
  0.6 9.0 %copy-start = (f32[1024,128]{1,0:T(8,128)S(1)}, f32[1024,128]{1,0:T(8,128)}, u32[]{:S(2)}) copy-start(f32[1024,128]{1,0:T(8,128)} %refs_1_.1) | copy-start | bytes 1572868
  0.6 9.0 %copy-start.1 = (f32[128,128]{1,0:T(8,128)S(1)}, f32[128,128]{1,0:T(8,128)}, u32[]{:S(2)}) copy-start(f32[128,128]{1,0:T(8,128)} %refs_3_.1) | copy-start | bytes 196612
  0.6 8.3 %collective-permute-start.2 = (f32[1024,128]{1,0:T(8,128)}, f32[1024,128]{1,0:T(8,128)S(1)}, u32[]{:S(2)}, u32[]{:S(2)}) collective-permute-start(f32[1024,128]{1,0:T(8,128)} %refs_1_.1), channel_id=1, source_target_pairs={{0,1},{1,0},{2,3},{3,2},{4,5},{5,4},{6,7},{7,6},{8,9},{9,8},{10,11... | collective-permute-start | bytes 1572872 | tf_op jit(solution)/shard_map/ppermute | solution.py:81
  1.2 15.1 %collective-permute-start.6 = (f32[1024,128]{1,0:T(8,128)}, f32[1024,128]{1,0:T(8,128)S(1)}, u32[]{:S(2)}, u32[]{:S(2)}) collective-permute-start(f32[1024,128]{1,0:T(8,128)} %refs_1_.1), channel_id=1, source_target_pairs={{0,3},{1,2},{2,1},{3,0},{4,7},{5,6},{6,5},{7,4},{8,11},{9,10},{10,... | collective-permute-start | bytes 1572872 | tf_op jit(solution)/shard_map/ppermute | solution.py:81
  3.8 5.2 %collective-permute-start = (f32[128,128]{1,0:T(8,128)}, f32[128,128]{1,0:T(8,128)S(1)}, u32[]{:S(2)}, u32[]{:S(2)}) collective-permute-start(f32[128,128]{1,0:T(8,128)} %refs_3_.1), channel_id=1, source_target_pairs={{0,8},{1,13},{2,10},{3,15},{4,12},{5,9},{6,14},{7,11},{8,0},{9,5},... | collective-permute-start | bytes 196616 | tf_op jit(solution)/shard_map/ppermute | solution.py:267
  5.4 7.1 %collective-permute-start.1 = (f32[128,128]{1,0:T(8,128)}, f32[128,128]{1,0:T(8,128)S(1)}, u32[]{:S(2)}, u32[]{:S(2)}) collective-permute-start(f32[128,128]{1,0:T(8,128)} %refs_3_.1), channel_id=1, source_target_pairs={{0,24},{1,29},{2,26},{3,31},{4,28},{5,25},{6,30},{7,27},{8,16},{9,... | collective-permute-start | bytes 196616 | tf_op jit(solution)/shard_map/ppermute | solution.py:267
  7.9 7.4 %collective-permute-start.4 = (f32[128,128]{1,0:T(8,128)}, f32[128,128]{1,0:T(8,128)S(1)}, u32[]{:S(2)}, u32[]{:S(2)}) collective-permute-start(f32[128,128]{1,0:T(8,128)} %refs_3_.1), channel_id=1, source_target_pairs={{0,16},{1,21},{2,18},{3,23},{4,20},{5,17},{6,22},{7,19},{8,24},{9,... | collective-permute-start | bytes 196616 | tf_op jit(solution)/shard_map/ppermute | solution.py:267
  10.4 4.0 %collective-permute-start.3 = (f32[64,128]{1,0:T(8,128)S(1)}, f32[64,128]{1,0:T(8,128)S(1)}, u32[]{:S(2)}, u32[]{:S(2)}) collective-permute-start(f32[64,128]{1,0:T(8,128)S(1)} %get-tuple-element.28), channel_id=1, source_target_pairs={{0,4},{4,0},{8,12},{12,8},{16,20},{20,16},{24,28},{28,24},{1,5},{5... | collective-permute-start | bytes 98312 | tf_op jit(solution)/shard_map/ppermute | solution.py:81
  16.2 2.4 %collective-permute-start.7 = (f32[1024,128]{1,0:T(8,128)S(1)}, f32[1024,128]{1,0:T(8,128)S(1)}, u32[]{:S(2)}, u32[]{:S(2)}) collective-permute-start(f32[1024,128]{1,0:T(8,128)S(1)} %collective-permute-done.6.refs_1_), channel_id=1, source_target_pairs={{0,1},{1,0},{2,3},{3,2},{4,5},{5,4},{6,7},{7,6},{8,9},{9,8},{10,11... | collective-permute-start | bytes 1572872 | tf_op jit(solution)/shard_map/ppermute | solution.py:81
  16.6 2.0 %collective-permute-start.5 = (f32[512,128]{1,0:T(8,128)S(1)}, f32[512,128]{1,0:T(8,128)S(1)}, u32[]{:S(2)}, u32[]{:S(2)}) collective-permute-start(f32[512,128]{1,0:T(8,128)S(1)} %constant_dynamic-update-slice_fusion.refs_0_.refs_1_), channel_id=1, source_target_pairs={{0,1},{1,0},{2,3},{3,2},{4,5},{5,4},{6,7},{7,6},{8,9},{9,8},{10,11... | collective-permute-start | bytes 786440 | tf_op jit(solution)/shard_map/ppermute | solution.py:81
  21.3 1.6 %collective-permute-start.8 = (f32[512,128]{1,0:T(8,128)S(1)}, f32[512,128]{1,0:T(8,128)S(1)}, u32[]{:S(2)}, u32[]{:S(2)}) collective-permute-start(f32[512,128]{1,0:T(8,128)S(1)} %get-tuple-element.39.refs_9_), channel_id=1, source_target_pairs={{0,1},{1,0},{2,3},{3,2},{4,5},{5,4},{6,7},{7,6},{8,9},{9,8},{10,11... | collective-permute-start | bytes 786440 | tf_op jit(solution)/shard_map/ppermute | solution.py:81

commit v6 on v5

--- a/solution.py
+++ b/solution.py
@@ -12,7 +12,7 @@
 
 step_size = 0.5
 LOG2E = 1.4426950408889634
-TILE = 1024
+TILE = 2048
 VMEM_BYTES = 48 << 20
 OVER_WIDTH = (((1,), (1,)), ((), ()))
 IN_VMEM = pl.BlockSpec(memory_space=pltpu.VMEM)
@@ -216,7 +216,7 @@
 
     for i in range(mine_ref.shape[0] // rows):
         mine_ref[pl.ds(i * rows, rows), :] = part((2 * i + core) * rows, rows)
-    half_ref[...] = part(core * half, half)
+    half_ref[...] = part((1 - core) * half, half)
     start_ref[...] = part(place * rows, rows)
 
 
@@ -287,7 +287,10 @@
         near, [(for_r, [references], [])], near_sum, cut=particles
     )
     at_hand = [mate_pair, own_pair]
-    beside = exchange(half, "dom", 1)
+    beside_pairs = [
+        (d * n_ref + r, (d ^ 1) * n_ref + (r ^ 1)) for d in range(n_dom) for r in range(n_ref)
+    ]
+    beside = lax.ppermute(half, ("dom", "ref"), beside_pairs)
     far_sum = pull(after(far, near_sum), [(for_r, [], at_hand)])[0]
     fourth = jnp.concatenate([mine, after(beside, far_sum)])
     fourth_sum = pull(fourth, [(for_r, [], at_hand)])[0]

time: 24.4 us -> 24.4 us (level)
    ppermute x0 -> x1, starting transfers between devices: none -> 0.97 us  [gather_plan(): beside = lax.ppermute(half, ('dom', 'ref'), beside_pairs)]
    ppermute x6 -> x5, starting transfers between devices: 4.96 us -> 4.11 us  [exchange(): return lax.ppermute(values, axis, [(i, i ^ offset) for i in range(size)])]
    ppermute x6 -> x5, waiting for transfers between devices: 1.04 us -> 0.19 us  [exchange(): return lax.ppermute(values, axis, [(i, i ^ offset) for i in range(size)])]
    ppermute x3, waiting for transfers between devices: 2.25 us -> 2.64 us  [by_core(): return lax.ppermute(values, ('dom', 'ref'), pairs)]
    ppermute x0 -> x1, waiting for transfers between devices: none -> 0.36 us  [gather_plan(): beside = lax.ppermute(half, ('dom', 'ref'), beside_pairs)]
  transfers between devices with their start and end apart: 9 -> 9, of which waited for: 4 -> 6; matrix products, arithmetic and copies ran while one was open for 0% -> 0% of each run, Pallas kernels for 29% -> 29%
where the time goes in v6:
time: 24.4 us; the launch traced here: 24.3 us
  Pallas kernels  11 us (45%)
  starting transfers between devices  9.25 us (38%)
  waiting for transfers between devices  3.18 us (13%)
  between operations  0.73 us (3%)
    pallas_call x9, Pallas kernels, pull(): pl.pallas_call(body, out_shape=outs, in_specs=[IN_VMEM] * len(args), out_...  11 us
    ppermute x3, starting transfers between devices, by_core(): return lax.ppermute(values, ('dom', 'ref'), pairs)  4.17 us
    ppermute x5, starting transfers between devices, exchange(): return lax.ppermute(values, axis, [(i, i ^ offset) for i in range(size)])  4.11 us
    ppermute x3, waiting for transfers between devices, by_core(): return lax.ppermute(values, ('dom', 'ref'), pairs)  2.64 us
    ppermute x1, starting transfers between devices, gather_plan(): beside = lax.ppermute(half, ('dom', 'ref'), beside_pairs)  0.97 us
  transfers between devices with their start and end apart: 9, of which 6 were waited for; matrix products, arithmetic and copies ran while one was open for 0% of the time, Pallas kernels for 29%

profile of v6, /device:TPU:0, one launch (start us, length us, event | category | flops | bytes accessed | tf_op | source)
XLA Modules:
  0.0 24.3 jit_solution(3571875249497120562)
XLA Ops:
  0.6 0.0 copy-start
  0.6 0.0 copy-start.1
  0.6 0.5 %collective-permute-start.2 = (f32[1024,128]{1,0:T(8,128)}, f32[1024,128]{1,0:T(8,128)S(1)}, u32[]{:S(2)}, u32[]{:S(2)}) collective-permute-start(f32[1024,128]{1,0:T(8,128)} %refs_1_.1), channel_id=1, source_target_pairs={{0,1},{1,0},{2,3},{3,2},{4,5},{5,4},{6,7},{7,6},{8,9},{9,8},{10,11... | collective-permute-start | bytes 1572872 | tf_op jit(solution)/shard_map/ppermute | solution.py:81
  1.2 2.6 %collective-permute-start.6 = (f32[1024,128]{1,0:T(8,128)}, f32[1024,128]{1,0:T(8,128)S(1)}, u32[]{:S(2)}, u32[]{:S(2)}) collective-permute-start(f32[1024,128]{1,0:T(8,128)} %refs_1_.1), channel_id=1, source_target_pairs={{0,3},{1,2},{2,1},{3,0},{4,7},{5,6},{6,5},{7,4},{8,11},{9,10},{10,... | collective-permute-start | bytes 1572872 | tf_op jit(solution)/shard_map/ppermute | solution.py:81
  3.8 1.6 %collective-permute-start = (f32[128,128]{1,0:T(8,128)}, f32[128,128]{1,0:T(8,128)S(1)}, u32[]{:S(2)}, u32[]{:S(2)}) collective-permute-start(f32[128,128]{1,0:T(8,128)} %refs_3_.1), channel_id=1, source_target_pairs={{0,8},{1,13},{2,10},{3,15},{4,12},{5,9},{6,14},{7,11},{8,0},{9,5},... | collective-permute-start | bytes 196616 | tf_op jit(solution)/shard_map/ppermute | solution.py:267
  5.4 2.5 %collective-permute-start.1 = (f32[128,128]{1,0:T(8,128)}, f32[128,128]{1,0:T(8,128)S(1)}, u32[]{:S(2)}, u32[]{:S(2)}) collective-permute-start(f32[128,128]{1,0:T(8,128)} %refs_3_.1), channel_id=1, source_target_pairs={{0,24},{1,29},{2,26},{3,31},{4,28},{5,25},{6,30},{7,27},{8,16},{9,... | collective-permute-start | bytes 196616 | tf_op jit(solution)/shard_map/ppermute | solution.py:267
  7.9 0.1 collective-permute-start.4
  8.0 1.0 %collective-permute-done.refs_0_ = f32[128,128]{1,0:T(8,128)S(1)} collective-permute-done((f32[128,128]{1,0:T(8,128)}, f32[128,128]{1,0:T(8,128)S(1)}, u32[]{:S(2)}, u32[]{:S(2)}) %collective-permute-start) | collective-permute-done | bytes 65568 | tf_op jit(solution)/shard_map/ppermute | solution.py:267
  9.0 0.0 collective-permute-done.2.refs_1_
  9.0 0.7 %shard_map.41 = (f32[128,128]{1,0:T(8,128)S(1)}, bf16[1024,256]{1,0:T(8,128)(2,1)S(1)}, f32[1,1024]{1,0:T(1,128)S(1)}) custom-call(f32[128,128]{1,0:T(8,128)S(1)} %collective-permute-done.refs_0_, f32[1024,128]{1,0:T(8,128)S(1)} %collective-permute-done.2.refs_1_), custom_call_target="tpu_custom_call" | custom-call | flops 1 | bytes 1 | tf_op jit(solution)/shard_map/pallas_call | solution.py:251
  9.7 0.0 copy-done
  9.7 0.0 copy-done.1
  9.7 0.7 %shard_map.42 = (f32[128,128]{1,0:T(8,128)S(1)}, f32[64,128]{1,0:T(8,128)S(1)}, f32[64,128]{1,0:T(8,128)S(1)}, f32[32,128]{1,0:T(8,128)S(1)}, bf16[1024,256]{1,0:T(8,128)(2,1)S(1)}, /*index=5*/f32[1,1024]{1,0:T(1,128)S(1)}) custom-call(f32[128,128]{1,0:T(8,128)S(1)} %collective-permute-done.refs_0_, f32[1024,128]{1,0:T(8,128)S(1)} %copy-done, ...), custom_call_target="tpu_custom_call" | custom-call | flops 1 | bytes 1 | tf_op jit(solution)/shard_map/pallas_call | solution.py:251
  10.4 1.0 %collective-permute-start.3 = (f32[64,128]{1,0:T(8,128)S(1)}, f32[64,128]{1,0:T(8,128)S(1)}, u32[]{:S(2)}, u32[]{:S(2)}) collective-permute-start(f32[64,128]{1,0:T(8,128)S(1)} %get-tuple-element.28), channel_id=1, source_target_pairs={{0,5},{1,4},{2,7},{3,6},{4,1},{5,0},{6,3},{7,2},{8,13},{9,12},{10,... | collective-permute-start | bytes 98312 | tf_op jit(solution)/shard_map/ppermute | solution.py:293
  11.3 1.2 %collective-permute-done.1.refs_0_ = f32[128,128]{1,0:T(8,128)S(1)} collective-permute-done((f32[128,128]{1,0:T(8,128)}, f32[128,128]{1,0:T(8,128)S(1)}, u32[]{:S(2)}, u32[]{:S(2)}) %collective-permute-start.1) | collective-permute-done | bytes 65568 | tf_op jit(solution)/shard_map/ppermute | solution.py:267
  12.5 0.9 %shard_map.43 = f32[128,128]{1,0:T(8,128)S(1)} custom-call(f32[128,128]{1,0:T(8,128)S(1)} %collective-permute-done.1.refs_0_, bf16[1024,256]{1,0:T(8,128)(2,1)S(1)} %get-tuple-element.31.refs_1_, f32[1,1024]{1,0:T(1,128)S(1)} %get-tuple-element.32.refs_2_, bf16[1024,256]{1,0:T(8,128)(2,1)S(1)} %get-tuple-element.33.refs_3_, ...), custom_call_target="tpu_custom_call" | custom-call | flops 1 | bytes 1 | tf_op jit(solution)/shard_map/pallas_call | solution.py:251
  13.4 0.4 %collective-permute-done.3 = f32[64,128]{1,0:T(8,128)S(1)} collective-permute-done((f32[64,128]{1,0:T(8,128)S(1)}, f32[64,128]{1,0:T(8,128)S(1)}, u32[]{:S(2)}, u32[]{:S(2)}) %collective-permute-start.3) | collective-permute-done | bytes 32800 | tf_op jit(solution)/shard_map/ppermute | solution.py:293
  13.8 0.9 %shard_map.44 = f32[128,128]{1,0:T(8,128)S(1)} custom-call(f32[128,128]{1,0:T(8,128)S(1)} %pad_maximum_fusion.1.refs_0_, bf16[1024,256]{1,0:T(8,128)(2,1)S(1)} %get-tuple-element.31.refs_1_, f32[1,1024]{1,0:T(1,128)S(1)} %get-tuple-element.32.refs_2_, bf16[1024,256]{1,0:T(8,128)(2,1)S(1)} %get-tuple-element.33.refs_3_, f32[1,1024]{1,0:T(1,128)S(1)} %get-tuple-element.34.refs_4_), custom_call_target="tpu_custom_call" | custom-call | flops 1 | bytes 1 | tf_op jit(solution)/shard_map/pallas_call | solution.py:251
  14.7 0.5 %collective-permute-done.4.refs_0_ = f32[128,128]{1,0:T(8,128)S(1)} collective-permute-done((f32[128,128]{1,0:T(8,128)}, f32[128,128]{1,0:T(8,128)S(1)}, u32[]{:S(2)}, u32[]{:S(2)}) %collective-permute-start.4) | collective-permute-done | bytes 65568 | tf_op jit(solution)/shard_map/ppermute | solution.py:267
  15.2 0.9 %shard_map.45 = f32[128,128]{1,0:T(8,128)S(1)} custom-call(f32[128,128]{1,0:T(8,128)S(1)} %collective-permute-done.4.refs_0_, bf16[1024,256]{1,0:T(8,128)(2,1)S(1)} %get-tuple-element.31.refs_1_, f32[1,1024]{1,0:T(1,128)S(1)} %get-tuple-element.32.refs_2_, bf16[1024,256]{1,0:T(8,128)(2,1)S(1)} %get-tuple-element.33.refs_3_, ...), custom_call_target="tpu_custom_call" | custom-call | flops 1 | bytes 1 | tf_op jit(solution)/shard_map/pallas_call | solution.py:251
  16.2 0.1 collective-permute-done.6.refs_1_
  16.2 0.4 %collective-permute-start.7 = (f32[1024,128]{1,0:T(8,128)S(1)}, f32[1024,128]{1,0:T(8,128)S(1)}, u32[]{:S(2)}, u32[]{:S(2)}) collective-permute-start(f32[1024,128]{1,0:T(8,128)S(1)} %collective-permute-done.6.refs_1_), channel_id=1, source_target_pairs={{0,1},{1,0},{2,3},{3,2},{4,5},{5,4},{6,7},{7,6},{8,9},{9,8},{10,11... | collective-permute-start | bytes 1572872 | tf_op jit(solution)/shard_map/ppermute | solution.py:81
  16.6 0.2 collective-permute-start.5
  16.9 1.6 %shard_map.46 = (f32[512,128]{1,0:T(8,128)S(1)}, bf16[1024,256]{1,0:T(8,128)(2,1)S(1)}, f32[1,1024]{1,0:T(1,128)S(1)}) custom-call(f32[512,128]{1,0:T(8,128)S(1)} %constant_dynamic-update-slice_fusion.refs_0_.refs_1_, f32[1024,128]{1,0:T(8,128)S(1)} %collective-permute-done.6.refs_1_, f32[512,128]{1,0:T(8,128)S(1)} %pad_maximum_fusion.refs_2_), custom_call_target="tpu_custom_call" | custom-call | flops 1 | bytes 1 | tf_op jit(solution)/shard_map/pallas_call | solution.py:251
  18.4 0.1 collective-permute-done.5.refs_2_
  18.5 0.0 collective-permute-done.7.refs_3_
  18.5 2.7 %shard_map.47 = (f32[512,128]{1,0:T(8,128)S(1)}, bf16[1024,256]{1,0:T(8,128)(2,1)}, f32[1,1024]{1,0:T(1,128)}, bf16[1024,256]{1,0:T(8,128)(2,1)S(1)}, f32[1,1024]{1,0:T(1,128)S(1)}) custom-call(f32[512,128]{1,0:T(8,128)S(1)} %constant_dynamic-update-slice_fusion.refs_0_.refs_1_, f32[512,128]{1,0:T(8,128)S(1)} %constant_dynamic-update-slice_fusion.refs_0_.refs_1_, ...), custom_call_target="tpu_custom_call" | custom-call | flops 1 | bytes 1 | tf_op jit(solution)/shard_map/pallas_call | solution.py:251
  21.3 0.4 %collective-permute-start.8 = (f32[512,128]{1,0:T(8,128)S(1)}, f32[512,128]{1,0:T(8,128)S(1)}, u32[]{:S(2)}, u32[]{:S(2)}) collective-permute-start(f32[512,128]{1,0:T(8,128)S(1)} %get-tuple-element.39.refs_9_), channel_id=1, source_target_pairs={{0,1},{1,0},{2,3},{3,2},{4,5},{5,4},{6,7},{7,6},{8,9},{9,8},{10,11... | collective-permute-start | bytes 786440 | tf_op jit(solution)/shard_map/ppermute | solution.py:81
  21.6 1.3 %shard_map.48 = (f32[32,128]{1,0:T(8,128)S(1)}, bf16[512,256]{1,0:T(8,128)(2,1)S(1)}, f32[1,512]{1,0:T(1,128)S(1)}) custom-call(f32[32,128]{1,0:T(8,128)S(1)} %constant_dynamic-slice_fusion.refs_0_, bf16[1024,256]{1,0:T(8,128)(2,1)S(1)} %get-tuple-element.31.refs_1_, f32[1,1024]{1,0:T(1,128)S(1)} %get-tuple-element.32.refs_2_, ...), custom_call_target="tpu_custom_call" | custom-call | flops 1 | bytes 1 | tf_op jit(solution)/shard_map/pallas_call | solution.py:251
  22.9 0.0 collective-permute-done.8.refs_1_
  22.9 1.3 %shard_map.49 = (f32[32,128]{1,0:T(8,128)}, f32[32,128]{1,0:T(8,128)}, bf16[512,256]{1,0:T(8,128)(2,1)}, f32[1,512]{1,0:T(1,128)}) custom-call(f32[32,128]{1,0:T(8,128)S(1)} %constant_dynamic-slice_fusion.refs_0_, f32[512,128]{1,0:T(8,128)S(1)} %collective-permute-done.8.refs_1_, bf16[512,256]{1,0:T(8,128)(2,1)S(1)} %get-tuple-element.44.refs_2_, ...), custom_call_target="tpu_custom_call" | custom-call | flops 1 | bytes 1 | tf_op jit(solution)/shard_map/pallas_call | solution.py:251
  (8 shorter events, 0.1 us)
Async XLA Ops:
  0.6 9.0 %copy-start = (f32[1024,128]{1,0:T(8,128)S(1)}, f32[1024,128]{1,0:T(8,128)}, u32[]{:S(2)}) copy-start(f32[1024,128]{1,0:T(8,128)} %refs_1_.1) | copy-start | bytes 1572868
  0.6 9.0 %copy-start.1 = (f32[128,128]{1,0:T(8,128)S(1)}, f32[128,128]{1,0:T(8,128)}, u32[]{:S(2)}) copy-start(f32[128,128]{1,0:T(8,128)} %refs_3_.1) | copy-start | bytes 196612
  0.6 8.3 %collective-permute-start.2 = (f32[1024,128]{1,0:T(8,128)}, f32[1024,128]{1,0:T(8,128)S(1)}, u32[]{:S(2)}, u32[]{:S(2)}) collective-permute-start(f32[1024,128]{1,0:T(8,128)} %refs_1_.1), channel_id=1, source_target_pairs={{0,1},{1,0},{2,3},{3,2},{4,5},{5,4},{6,7},{7,6},{8,9},{9,8},{10,11... | collective-permute-start | bytes 1572872 | tf_op jit(solution)/shard_map/ppermute | solution.py:81
  1.2 15.1 %collective-permute-start.6 = (f32[1024,128]{1,0:T(8,128)}, f32[1024,128]{1,0:T(8,128)S(1)}, u32[]{:S(2)}, u32[]{:S(2)}) collective-permute-start(f32[1024,128]{1,0:T(8,128)} %refs_1_.1), channel_id=1, source_target_pairs={{0,3},{1,2},{2,1},{3,0},{4,7},{5,6},{6,5},{7,4},{8,11},{9,10},{10,... | collective-permute-start | bytes 1572872 | tf_op jit(solution)/shard_map/ppermute | solution.py:81
  3.8 5.2 %collective-permute-start = (f32[128,128]{1,0:T(8,128)}, f32[128,128]{1,0:T(8,128)S(1)}, u32[]{:S(2)}, u32[]{:S(2)}) collective-permute-start(f32[128,128]{1,0:T(8,128)} %refs_3_.1), channel_id=1, source_target_pairs={{0,8},{1,13},{2,10},{3,15},{4,12},{5,9},{6,14},{7,11},{8,0},{9,5},... | collective-permute-start | bytes 196616 | tf_op jit(solution)/shard_map/ppermute | solution.py:267
  5.4 7.1 %collective-permute-start.1 = (f32[128,128]{1,0:T(8,128)}, f32[128,128]{1,0:T(8,128)S(1)}, u32[]{:S(2)}, u32[]{:S(2)}) collective-permute-start(f32[128,128]{1,0:T(8,128)} %refs_3_.1), channel_id=1, source_target_pairs={{0,24},{1,29},{2,26},{3,31},{4,28},{5,25},{6,30},{7,27},{8,16},{9,... | collective-permute-start | bytes 196616 | tf_op jit(solution)/shard_map/ppermute | solution.py:267
  7.9 7.4 %collective-permute-start.4 = (f32[128,128]{1,0:T(8,128)}, f32[128,128]{1,0:T(8,128)S(1)}, u32[]{:S(2)}, u32[]{:S(2)}) collective-permute-start(f32[128,128]{1,0:T(8,128)} %refs_3_.1), channel_id=1, source_target_pairs={{0,16},{1,21},{2,18},{3,23},{4,20},{5,17},{6,22},{7,19},{8,24},{9,... | collective-permute-start | bytes 196616 | tf_op jit(solution)/shard_map/ppermute | solution.py:267
  10.4 3.4 %collective-permute-start.3 = (f32[64,128]{1,0:T(8,128)S(1)}, f32[64,128]{1,0:T(8,128)S(1)}, u32[]{:S(2)}, u32[]{:S(2)}) collective-permute-start(f32[64,128]{1,0:T(8,128)S(1)} %get-tuple-element.28), channel_id=1, source_target_pairs={{0,5},{1,4},{2,7},{3,6},{4,1},{5,0},{6,3},{7,2},{8,13},{9,12},{10,... | collective-permute-start | bytes 98312 | tf_op jit(solution)/shard_map/ppermute | solution.py:293
  16.2 2.3 %collective-permute-start.7 = (f32[1024,128]{1,0:T(8,128)S(1)}, f32[1024,128]{1,0:T(8,128)S(1)}, u32[]{:S(2)}, u32[]{:S(2)}) collective-permute-start(f32[1024,128]{1,0:T(8,128)S(1)} %collective-permute-done.6.refs_1_), channel_id=1, source_target_pairs={{0,1},{1,0},{2,3},{3,2},{4,5},{5,4},{6,7},{7,6},{8,9},{9,8},{10,11... | collective-permute-start | bytes 1572872 | tf_op jit(solution)/shard_map/ppermute | solution.py:81
  16.6 1.9 %collective-permute-start.5 = (f32[512,128]{1,0:T(8,128)S(1)}, f32[512,128]{1,0:T(8,128)S(1)}, u32[]{:S(2)}, u32[]{:S(2)}) collective-permute-start(f32[512,128]{1,0:T(8,128)S(1)} %constant_dynamic-update-slice_fusion.refs_0_.refs_1_), channel_id=1, source_target_pairs={{0,1},{1,0},{2,3},{3,2},{4,5},{5,4},{6,7},{7,6},{8,9},{9,8},{10,11... | collective-permute-start | bytes 786440 | tf_op jit(solution)/shard_map/ppermute | solution.py:81
  21.3 1.6 %collective-permute-start.8 = (f32[512,128]{1,0:T(8,128)S(1)}, f32[512,128]{1,0:T(8,128)S(1)}, u32[]{:S(2)}, u32[]{:S(2)}) collective-permute-start(f32[512,128]{1,0:T(8,128)S(1)} %get-tuple-element.39.refs_9_), channel_id=1, source_target_pairs={{0,1},{1,0},{2,3},{3,2},{4,5},{5,4},{6,7},{7,6},{8,9},{9,8},{10,11... | collective-permute-start | bytes 786440 | tf_op jit(solution)/shard_map/ppermute | solution.py:81

commit v7 on v6

--- a/solution.py
+++ b/solution.py
@@ -303,8 +303,8 @@
     across = after(across, middle_sum)
     across_mate = exchange(across, "ref", 1)
     held_sum, across_pair = pull(held, [(for_r, [across], [])], held_sum)
-    groups = [(for_p, [held, held_by_mate], []), (for_r, [across_mate], [])]
-    moved, _, across_mate_pair = pull(held, groups, held_sum, moves=True)
+    groups = [(for_r, [across_mate], []), (for_p, [held, held_by_mate], [])]
+    moved, across_mate_pair, _ = pull(held, groups, held_sum, moves=True)
 
     moved_by_mate = exchange(moved, "ref", 1)
     own_rows = lax.dynamic_slice_in_dim(moved, 2 * block_rows + (place // 2) * rows, rows, 0)

time: 24.4 us -> 24.4 us (level)
  no operation moved by 1% of the time
where the time goes in v7:
time: 24.4 us; the launch traced here: 24.2 us
  Pallas kernels  11 us (45%)
  starting transfers between devices  9.24 us (38%)
  waiting for transfers between devices  3.18 us (13%)
  between operations  0.73 us (3%)
    pallas_call x9, Pallas kernels, pull(): pl.pallas_call(body, out_shape=outs, in_specs=[IN_VMEM] * len(args), out_...  11 us
    ppermute x3, starting transfers between devices, by_core(): return lax.ppermute(values, ('dom', 'ref'), pairs)  4.17 us
    ppermute x5, starting transfers between devices, exchange(): return lax.ppermute(values, axis, [(i, i ^ offset) for i in range(size)])  4.11 us
    ppermute x3, waiting for transfers between devices, by_core(): return lax.ppermute(values, ('dom', 'ref'), pairs)  2.64 us
    ppermute x1, starting transfers between devices, gather_plan(): beside = lax.ppermute(half, ('dom', 'ref'), beside_pairs)  0.97 us
  transfers between devices with their start and end apart: 9, of which 6 were waited for; matrix products, arithmetic and copies ran while one was open for 0% of the time, Pallas kernels for 29%

profile of v7, /device:TPU:0, one launch (start us, length us, event | category | flops | bytes accessed | tf_op | source)
XLA Modules:
  0.0 24.2 jit_solution(1999448054626584045)
XLA Ops:
  0.6 0.0 copy-start
  0.6 0.0 copy-start.1
  0.6 0.5 %collective-permute-start.2 = (f32[1024,128]{1,0:T(8,128)}, f32[1024,128]{1,0:T(8,128)S(1)}, u32[]{:S(2)}, u32[]{:S(2)}) collective-permute-start(f32[1024,128]{1,0:T(8,128)} %refs_1_.1), channel_id=1, source_target_pairs={{0,1},{1,0},{2,3},{3,2},{4,5},{5,4},{6,7},{7,6},{8,9},{9,8},{10,11... | collective-permute-start | bytes 1572872 | tf_op jit(solution)/shard_map/ppermute | solution.py:81
  1.2 2.6 %collective-permute-start.5 = (f32[1024,128]{1,0:T(8,128)}, f32[1024,128]{1,0:T(8,128)S(1)}, u32[]{:S(2)}, u32[]{:S(2)}) collective-permute-start(f32[1024,128]{1,0:T(8,128)} %refs_1_.1), channel_id=1, source_target_pairs={{0,3},{1,2},{2,1},{3,0},{4,7},{5,6},{6,5},{7,4},{8,11},{9,10},{10,... | collective-permute-start | bytes 1572872 | tf_op jit(solution)/shard_map/ppermute | solution.py:81
  3.8 1.6 %collective-permute-start = (f32[128,128]{1,0:T(8,128)}, f32[128,128]{1,0:T(8,128)S(1)}, u32[]{:S(2)}, u32[]{:S(2)}) collective-permute-start(f32[128,128]{1,0:T(8,128)} %refs_3_.1), channel_id=1, source_target_pairs={{0,8},{1,13},{2,10},{3,15},{4,12},{5,9},{6,14},{7,11},{8,0},{9,5},... | collective-permute-start | bytes 196616 | tf_op jit(solution)/shard_map/ppermute | solution.py:267
  5.4 2.5 %collective-permute-start.1 = (f32[128,128]{1,0:T(8,128)}, f32[128,128]{1,0:T(8,128)S(1)}, u32[]{:S(2)}, u32[]{:S(2)}) collective-permute-start(f32[128,128]{1,0:T(8,128)} %refs_3_.1), channel_id=1, source_target_pairs={{0,24},{1,29},{2,26},{3,31},{4,28},{5,25},{6,30},{7,27},{8,16},{9,... | collective-permute-start | bytes 196616 | tf_op jit(solution)/shard_map/ppermute | solution.py:267
  7.9 0.1 collective-permute-start.4
  8.0 1.0 %collective-permute-done.refs_0_ = f32[128,128]{1,0:T(8,128)S(1)} collective-permute-done((f32[128,128]{1,0:T(8,128)}, f32[128,128]{1,0:T(8,128)S(1)}, u32[]{:S(2)}, u32[]{:S(2)}) %collective-permute-start) | collective-permute-done | bytes 65568 | tf_op jit(solution)/shard_map/ppermute | solution.py:267
  9.0 0.0 collective-permute-done.2.refs_1_
  9.0 0.7 %shard_map.41 = (f32[128,128]{1,0:T(8,128)S(1)}, bf16[1024,256]{1,0:T(8,128)(2,1)S(1)}, f32[1,1024]{1,0:T(1,128)S(1)}) custom-call(f32[128,128]{1,0:T(8,128)S(1)} %collective-permute-done.refs_0_, f32[1024,128]{1,0:T(8,128)S(1)} %collective-permute-done.2.refs_1_), custom_call_target="tpu_custom_call" | custom-call | flops 1 | bytes 1 | tf_op jit(solution)/shard_map/pallas_call | solution.py:251
  9.7 0.0 copy-done
  9.7 0.0 copy-done.1
  9.7 0.7 %shard_map.42 = (f32[128,128]{1,0:T(8,128)S(1)}, f32[64,128]{1,0:T(8,128)S(1)}, f32[64,128]{1,0:T(8,128)S(1)}, f32[32,128]{1,0:T(8,128)S(1)}, bf16[1024,256]{1,0:T(8,128)(2,1)S(1)}, /*index=5*/f32[1,1024]{1,0:T(1,128)S(1)}) custom-call(f32[128,128]{1,0:T(8,128)S(1)} %collective-permute-done.refs_0_, f32[1024,128]{1,0:T(8,128)S(1)} %copy-done, ...), custom_call_target="tpu_custom_call" | custom-call | flops 1 | bytes 1 | tf_op jit(solution)/shard_map/pallas_call | solution.py:251
  10.4 1.0 %collective-permute-start.3 = (f32[64,128]{1,0:T(8,128)S(1)}, f32[64,128]{1,0:T(8,128)S(1)}, u32[]{:S(2)}, u32[]{:S(2)}) collective-permute-start(f32[64,128]{1,0:T(8,128)S(1)} %get-tuple-element.28), channel_id=1, source_target_pairs={{0,5},{1,4},{2,7},{3,6},{4,1},{5,0},{6,3},{7,2},{8,13},{9,12},{10,... | collective-permute-start | bytes 98312 | tf_op jit(solution)/shard_map/ppermute | solution.py:293
  11.3 1.2 %collective-permute-done.1.refs_0_ = f32[128,128]{1,0:T(8,128)S(1)} collective-permute-done((f32[128,128]{1,0:T(8,128)}, f32[128,128]{1,0:T(8,128)S(1)}, u32[]{:S(2)}, u32[]{:S(2)}) %collective-permute-start.1) | collective-permute-done | bytes 65568 | tf_op jit(solution)/shard_map/ppermute | solution.py:267
  12.5 0.9 %shard_map.43 = f32[128,128]{1,0:T(8,128)S(1)} custom-call(f32[128,128]{1,0:T(8,128)S(1)} %collective-permute-done.1.refs_0_, bf16[1024,256]{1,0:T(8,128)(2,1)S(1)} %get-tuple-element.31.refs_1_, f32[1,1024]{1,0:T(1,128)S(1)} %get-tuple-element.32.refs_2_, bf16[1024,256]{1,0:T(8,128)(2,1)S(1)} %get-tuple-element.33.refs_3_, ...), custom_call_target="tpu_custom_call" | custom-call | flops 1 | bytes 1 | tf_op jit(solution)/shard_map/pallas_call | solution.py:251
  13.4 0.4 %collective-permute-done.3 = f32[64,128]{1,0:T(8,128)S(1)} collective-permute-done((f32[64,128]{1,0:T(8,128)S(1)}, f32[64,128]{1,0:T(8,128)S(1)}, u32[]{:S(2)}, u32[]{:S(2)}) %collective-permute-start.3) | collective-permute-done | bytes 32800 | tf_op jit(solution)/shard_map/ppermute | solution.py:293
  13.8 0.9 %shard_map.44 = f32[128,128]{1,0:T(8,128)S(1)} custom-call(f32[128,128]{1,0:T(8,128)S(1)} %pad_maximum_fusion.1.refs_0_, bf16[1024,256]{1,0:T(8,128)(2,1)S(1)} %get-tuple-element.31.refs_1_, f32[1,1024]{1,0:T(1,128)S(1)} %get-tuple-element.32.refs_2_, bf16[1024,256]{1,0:T(8,128)(2,1)S(1)} %get-tuple-element.33.refs_3_, f32[1,1024]{1,0:T(1,128)S(1)} %get-tuple-element.34.refs_4_), custom_call_target="tpu_custom_call" | custom-call | flops 1 | bytes 1 | tf_op jit(solution)/shard_map/pallas_call | solution.py:251
  14.7 0.5 %collective-permute-done.4.refs_0_ = f32[128,128]{1,0:T(8,128)S(1)} collective-permute-done((f32[128,128]{1,0:T(8,128)}, f32[128,128]{1,0:T(8,128)S(1)}, u32[]{:S(2)}, u32[]{:S(2)}) %collective-permute-start.4) | collective-permute-done | bytes 65568 | tf_op jit(solution)/shard_map/ppermute | solution.py:267
  15.2 0.9 %shard_map.45 = f32[128,128]{1,0:T(8,128)S(1)} custom-call(f32[128,128]{1,0:T(8,128)S(1)} %collective-permute-done.4.refs_0_, bf16[1024,256]{1,0:T(8,128)(2,1)S(1)} %get-tuple-element.31.refs_1_, f32[1,1024]{1,0:T(1,128)S(1)} %get-tuple-element.32.refs_2_, bf16[1024,256]{1,0:T(8,128)(2,1)S(1)} %get-tuple-element.33.refs_3_, ...), custom_call_target="tpu_custom_call" | custom-call | flops 1 | bytes 1 | tf_op jit(solution)/shard_map/pallas_call | solution.py:251
  16.2 0.1 collective-permute-done.5.refs_1_
  16.2 0.4 %collective-permute-start.6 = (f32[1024,128]{1,0:T(8,128)S(1)}, f32[1024,128]{1,0:T(8,128)S(1)}, u32[]{:S(2)}, u32[]{:S(2)}) collective-permute-start(f32[1024,128]{1,0:T(8,128)S(1)} %collective-permute-done.5.refs_1_), channel_id=1, source_target_pairs={{0,1},{1,0},{2,3},{3,2},{4,5},{5,4},{6,7},{7,6},{8,9},{9,8},{10,11... | collective-permute-start | bytes 1572872 | tf_op jit(solution)/shard_map/ppermute | solution.py:81
  16.6 0.2 collective-permute-start.7
  16.9 1.6 %shard_map.46 = (f32[512,128]{1,0:T(8,128)S(1)}, bf16[1024,256]{1,0:T(8,128)(2,1)S(1)}, f32[1,1024]{1,0:T(1,128)S(1)}) custom-call(f32[512,128]{1,0:T(8,128)S(1)} %constant_dynamic-update-slice_fusion.refs_0_.refs_2_, f32[1024,128]{1,0:T(8,128)S(1)} %collective-permute-done.5.refs_1_, f32[512,128]{1,0:T(8,128)S(1)} %pad_maximum_fusion.refs_2_), custom_call_target="tpu_custom_call" | custom-call | flops 1 | bytes 1 | tf_op jit(solution)/shard_map/pallas_call | solution.py:251
  18.4 0.1 collective-permute-done.7.refs_3_
  18.5 0.0 collective-permute-done.6.refs_1_
  18.5 2.7 %shard_map.47 = (f32[512,128]{1,0:T(8,128)S(1)}, bf16[1024,256]{1,0:T(8,128)(2,1)S(1)}, f32[1,1024]{1,0:T(1,128)S(1)}, bf16[1024,256]{1,0:T(8,128)(2,1)}, f32[1,1024]{1,0:T(1,128)}) custom-call(f32[512,128]{1,0:T(8,128)S(1)} %constant_dynamic-update-slice_fusion.refs_0_.refs_2_, f32[1024,128]{1,0:T(8,128)S(1)} %collective-permute-done.6.refs_1_, ...), custom_call_target="tpu_custom_call" | custom-call | flops 1 | bytes 1 | tf_op jit(solution)/shard_map/pallas_call | solution.py:251
  21.3 0.4 %collective-permute-start.8 = (f32[512,128]{1,0:T(8,128)S(1)}, f32[512,128]{1,0:T(8,128)S(1)}, u32[]{:S(2)}, u32[]{:S(2)}) collective-permute-start(f32[512,128]{1,0:T(8,128)S(1)} %get-tuple-element.39.refs_9_), channel_id=1, source_target_pairs={{0,1},{1,0},{2,3},{3,2},{4,5},{5,4},{6,7},{7,6},{8,9},{9,8},{10,11... | collective-permute-start | bytes 786440 | tf_op jit(solution)/shard_map/ppermute | solution.py:81
  21.6 1.3 %shard_map.48 = (f32[32,128]{1,0:T(8,128)S(1)}, bf16[512,256]{1,0:T(8,128)(2,1)S(1)}, f32[1,512]{1,0:T(1,128)S(1)}) custom-call(f32[32,128]{1,0:T(8,128)S(1)} %constant_dynamic-slice_fusion.refs_0_, bf16[1024,256]{1,0:T(8,128)(2,1)S(1)} %get-tuple-element.31.refs_1_, f32[1,1024]{1,0:T(1,128)S(1)} %get-tuple-element.32.refs_2_, ...), custom_call_target="tpu_custom_call" | custom-call | flops 1 | bytes 1 | tf_op jit(solution)/shard_map/pallas_call | solution.py:251
  22.9 0.0 collective-permute-done.8.refs_1_
  22.9 1.3 %shard_map.49 = (f32[32,128]{1,0:T(8,128)}, f32[32,128]{1,0:T(8,128)}, bf16[512,256]{1,0:T(8,128)(2,1)}, f32[1,512]{1,0:T(1,128)}) custom-call(f32[32,128]{1,0:T(8,128)S(1)} %constant_dynamic-slice_fusion.refs_0_, f32[512,128]{1,0:T(8,128)S(1)} %collective-permute-done.8.refs_1_, bf16[512,256]{1,0:T(8,128)(2,1)S(1)} %get-tuple-element.44.refs_2_, ...), custom_call_target="tpu_custom_call" | custom-call | flops 1 | bytes 1 | tf_op jit(solution)/shard_map/pallas_call | solution.py:251
  (8 shorter events, 0.1 us)
Async XLA Ops:
  0.6 9.0 %copy-start = (f32[1024,128]{1,0:T(8,128)S(1)}, f32[1024,128]{1,0:T(8,128)}, u32[]{:S(2)}) copy-start(f32[1024,128]{1,0:T(8,128)} %refs_1_.1) | copy-start | bytes 1572868
  0.6 9.0 %copy-start.1 = (f32[128,128]{1,0:T(8,128)S(1)}, f32[128,128]{1,0:T(8,128)}, u32[]{:S(2)}) copy-start(f32[128,128]{1,0:T(8,128)} %refs_3_.1) | copy-start | bytes 196612
  0.6 8.3 %collective-permute-start.2 = (f32[1024,128]{1,0:T(8,128)}, f32[1024,128]{1,0:T(8,128)S(1)}, u32[]{:S(2)}, u32[]{:S(2)}) collective-permute-start(f32[1024,128]{1,0:T(8,128)} %refs_1_.1), channel_id=1, source_target_pairs={{0,1},{1,0},{2,3},{3,2},{4,5},{5,4},{6,7},{7,6},{8,9},{9,8},{10,11... | collective-permute-start | bytes 1572872 | tf_op jit(solution)/shard_map/ppermute | solution.py:81
  1.2 15.1 %collective-permute-start.5 = (f32[1024,128]{1,0:T(8,128)}, f32[1024,128]{1,0:T(8,128)S(1)}, u32[]{:S(2)}, u32[]{:S(2)}) collective-permute-start(f32[1024,128]{1,0:T(8,128)} %refs_1_.1), channel_id=1, source_target_pairs={{0,3},{1,2},{2,1},{3,0},{4,7},{5,6},{6,5},{7,4},{8,11},{9,10},{10,... | collective-permute-start | bytes 1572872 | tf_op jit(solution)/shard_map/ppermute | solution.py:81
  3.8 5.2 %collective-permute-start = (f32[128,128]{1,0:T(8,128)}, f32[128,128]{1,0:T(8,128)S(1)}, u32[]{:S(2)}, u32[]{:S(2)}) collective-permute-start(f32[128,128]{1,0:T(8,128)} %refs_3_.1), channel_id=1, source_target_pairs={{0,8},{1,13},{2,10},{3,15},{4,12},{5,9},{6,14},{7,11},{8,0},{9,5},... | collective-permute-start | bytes 196616 | tf_op jit(solution)/shard_map/ppermute | solution.py:267
  5.4 7.1 %collective-permute-start.1 = (f32[128,128]{1,0:T(8,128)}, f32[128,128]{1,0:T(8,128)S(1)}, u32[]{:S(2)}, u32[]{:S(2)}) collective-permute-start(f32[128,128]{1,0:T(8,128)} %refs_3_.1), channel_id=1, source_target_pairs={{0,24},{1,29},{2,26},{3,31},{4,28},{5,25},{6,30},{7,27},{8,16},{9,... | collective-permute-start | bytes 196616 | tf_op jit(solution)/shard_map/ppermute | solution.py:267
  7.9 7.4 %collective-permute-start.4 = (f32[128,128]{1,0:T(8,128)}, f32[128,128]{1,0:T(8,128)S(1)}, u32[]{:S(2)}, u32[]{:S(2)}) collective-permute-start(f32[128,128]{1,0:T(8,128)} %refs_3_.1), channel_id=1, source_target_pairs={{0,16},{1,21},{2,18},{3,23},{4,20},{5,17},{6,22},{7,19},{8,24},{9,... | collective-permute-start | bytes 196616 | tf_op jit(solution)/shard_map/ppermute | solution.py:267
  10.4 3.4 %collective-permute-start.3 = (f32[64,128]{1,0:T(8,128)S(1)}, f32[64,128]{1,0:T(8,128)S(1)}, u32[]{:S(2)}, u32[]{:S(2)}) collective-permute-start(f32[64,128]{1,0:T(8,128)S(1)} %get-tuple-element.28), channel_id=1, source_target_pairs={{0,5},{1,4},{2,7},{3,6},{4,1},{5,0},{6,3},{7,2},{8,13},{9,12},{10,... | collective-permute-start | bytes 98312 | tf_op jit(solution)/shard_map/ppermute | solution.py:293
  16.2 2.3 %collective-permute-start.6 = (f32[1024,128]{1,0:T(8,128)S(1)}, f32[1024,128]{1,0:T(8,128)S(1)}, u32[]{:S(2)}, u32[]{:S(2)}) collective-permute-start(f32[1024,128]{1,0:T(8,128)S(1)} %collective-permute-done.5.refs_1_), channel_id=1, source_target_pairs={{0,1},{1,0},{2,3},{3,2},{4,5},{5,4},{6,7},{7,6},{8,9},{9,8},{10,11... | collective-permute-start | bytes 1572872 | tf_op jit(solution)/shard_map/ppermute | solution.py:81
  16.6 1.9 %collective-permute-start.7 = (f32[512,128]{1,0:T(8,128)S(1)}, f32[512,128]{1,0:T(8,128)S(1)}, u32[]{:S(2)}, u32[]{:S(2)}) collective-permute-start(f32[512,128]{1,0:T(8,128)S(1)} %constant_dynamic-update-slice_fusion.refs_0_.refs_2_), channel_id=1, source_target_pairs={{0,1},{1,0},{2,3},{3,2},{4,5},{5,4},{6,7},{7,6},{8,9},{9,8},{10,11... | collective-permute-start | bytes 786440 | tf_op jit(solution)/shard_map/ppermute | solution.py:81
  21.3 1.6 %collective-permute-start.8 = (f32[512,128]{1,0:T(8,128)S(1)}, f32[512,128]{1,0:T(8,128)S(1)}, u32[]{:S(2)}, u32[]{:S(2)}) collective-permute-start(f32[512,128]{1,0:T(8,128)S(1)} %get-tuple-element.39.refs_9_), channel_id=1, source_target_pairs={{0,1},{1,0},{2,3},{3,2},{4,5},{5,4},{6,7},{7,6},{8,9},{9,8},{10,11... | collective-permute-start | bytes 786440 | tf_op jit(solution)/shard_map/ppermute | solution.py:81
